TPU v7x, 128 devices: a whole 4x4x4 slice. The times are simulated.
128 devices in a mesh: tile: 4 (over x), block: 32 (over y, z, core).
Axes of the slice: x: 4, y: 4, z: 4, core: 2. Of those that a mesh axis runs over, the one named last changes fastest.
Arguments:
- samples: bfloat16 [393216, 1024], P(('tile', 'block')), may hold values from -24 to 24
- shot_id: int32 [393216], P(('tile', 'block')), may hold values from 0 to 1023, as said below
- recv_id: int32 [393216], P(('tile', 'block')), may hold values from 0 to 2047, as said below
- shot_owner: int32 [1024], replicated, may hold values from 0 to 1023, as said below
- recv_owner: int32 [2048], replicated, may hold values from 0 to 2047, as said below
- counts: int32 [128], P(('tile', 'block')), may hold values from 1 to 3072, 157286 in all
Outputs:
- shot_terms: float32 [1024, 513], P(('tile', 'block'))
- receiver_terms: float32 [2048, 513], P(('tile', 'block'))
- residual: float32 [393216, 513], P(('tile', 'block'))
Inputs may be any that keep to these rules, and one draw needn't show every extreme that they name: Each device's live traces fill its first counts slots; the largest count is 3072. `shot_id`: A trace slot of device d (of N devices) records a shot of one of two swaths of 56 shots: the one that starts at (d - 3) * 8 and the one that starts at (d + N / 2 - 3) * 8, counted modulo 1024; each device's slots name every shot of both swaths. `recv_id`: A trace slot of device d (of N devices) records a receiver of one of two swaths of 112 receivers: the one that starts at (d - 3) * 16 and the one that starts at (d + N / 2 - 3) * 16, counted modulo 2048; each device's slots name every receiver of both swaths. `shot_owner`: A permutation of the shot term table's rows that keeps each shot s in rows of owner s // 8. `recv_owner`: A permutation of the receiver term table's rows that keeps each receiver r in rows of owner r // 16.
All inputs are finite; a program needn't handle non-finite values.
Results may differ from a plain program's by a relative error of at most 0.0039.
Values sent between devices are 32-bit elements; how exact they have to be, the bound alone decides.
A program may use at most 128 MiB of HBM per device.

v0:
```python
import math

import jax
import jax.numpy as jnp
from jax import lax
from jax.sharding import PartitionSpec as P

SWEEPS = 2


FLOOR = 0.05
DAMP = 1.0


def dft_basis(nsamp):
    half = nsamp // 2 + 1
    freq = jnp.arange(half, dtype=jnp.int32)
    sample = jnp.arange(nsamp, dtype=jnp.int32)
    phase = sample[:, None] * freq[None, :] % nsamp
    angle = phase.astype(jnp.float32) * (2.0 * math.pi / nsamp)
    norm = 1.0 / math.sqrt(nsamp)
    basis = jnp.concatenate([jnp.cos(angle) * norm, -jnp.sin(angle) * norm], axis=1)
    return basis.astype(jnp.bfloat16)


def settle_shots(partial_value, tally):
    mine_sum, mine_tally = (
        lax.psum_scatter(partial_value, ("tile", "block"), scatter_dimension=0, tiled=True),
        lax.psum_scatter(tally, ("tile", "block"), scatter_dimension=0, tiled=True),
    )
    mine = mine_sum / (mine_tally[:, None] + DAMP)
    whole = lax.all_gather(mine, ("tile", "block"), axis=0, tiled=True)
    return (mine, whole)


def settle_receivers(partial_value, tally):
    mine_sum, mine_tally = (
        lax.psum_scatter(partial_value, ("tile", "block"), scatter_dimension=0, tiled=True),
        lax.psum_scatter(tally, ("tile", "block"), scatter_dimension=0, tiled=True),
    )
    mine = mine_sum / (mine_tally[:, None] + DAMP)
    whole = lax.all_gather(mine, ("tile", "block"), axis=0, tiled=True)
    return (mine, whole)


def shards(samples, shot_id, recv_id, shot_owner, recv_owner, counts):
    rows = samples.shape[0]
    nsamp = samples.shape[1]
    bins = nsamp // 2 + 1
    nshots = shot_owner.shape[0]
    nrecv = recv_owner.shape[0]
    devices = lax.axis_size(("tile", "block"))
    shot_owned = nshots // devices
    recv_owned = nrecv // devices
    basis = dft_basis(nsamp)
    spectrum = jnp.dot(samples, basis, preferred_element_type=jnp.float32)
    real_part = spectrum[:, :bins]
    imag_part = spectrum[:, bins:]
    log_power = jnp.log(real_part * real_part + imag_part * imag_part + FLOOR)
    slot_index = jnp.arange(rows, dtype=jnp.int32)
    alive = (slot_index < counts[0]).astype(jnp.float32)
    shot_row = jnp.take(shot_owner, shot_id)
    recv_row = jnp.take(recv_owner, recv_id)
    weighted = alive[:, None] * log_power
    shot_tally = jax.ops.segment_sum(alive, shot_row, num_segments=nshots)
    recv_tally = jax.ops.segment_sum(alive, recv_row, num_segments=nrecv)
    recv_whole = jnp.zeros((nrecv, bins), jnp.float32)
    shot_whole = jnp.zeros((nshots, bins), jnp.float32)
    shot_mine = jnp.zeros((shot_owned, bins), jnp.float32)
    recv_mine = jnp.zeros((recv_owned, bins), jnp.float32)
    for sweep in range(SWEEPS):
        resid = weighted - alive[:, None] * jnp.take(recv_whole, recv_row, axis=0)
        partial_value = jax.ops.segment_sum(resid, shot_row, num_segments=nshots)
        shot_mine, shot_whole = settle_shots(partial_value, shot_tally)
        resid = weighted - alive[:, None] * jnp.take(shot_whole, shot_row, axis=0)
        partial_value = jax.ops.segment_sum(resid, recv_row, num_segments=nrecv)
        recv_mine, recv_whole = settle_receivers(partial_value, recv_tally)
    residual = alive[:, None] * (
        log_power - jnp.take(shot_whole, shot_row, axis=0) - jnp.take(recv_whole, recv_row, axis=0)
    )
    return (shot_mine, recv_mine, residual)


def solution(mesh):
    return jax.shard_map(
        shards,
        mesh=mesh,
        in_specs=(
            P(("tile", "block"), None),
            P(("tile", "block")),
            P(("tile", "block")),
            P(),
            P(),
            P(("tile", "block")),
        ),
        out_specs=(
            P(("tile", "block"), None),
            P(("tile", "block"), None),
            P(("tile", "block"), None),
        ),
        check_vma=False,
    )
```

profile of v0, /device:TPU:1, one launch (start us, length us, event | category | flops | bytes accessed | tf_op | source)
XLA Modules:
  0.0 2225.2 jit_solution(17851764799740379313)
XLA Ops:
  7.2 10.8 multiply_convert_fusion
  18.7 0.7 fusion.25
  19.4 12.6 gather_fusion
  32.1 17.4 gather_fusion.1
  49.6 2.7 broadcast.46
  52.3 16.9 gather_fusion.2
  69.2 8.5 copy.23
  77.7 11.3 convolution_bitcast_fusion
  88.9 6.1 fusion.6
  95.0 8.2 copy.24
  103.2 22.7 %scatter_custom_fusion = f32[1024,513]{1,0:T(8,128)} fusion(s32[3072]{0:T(1024)S(1)} %get-tuple-element.8, f32[3072,513]{1,0:T(8,128)} %copy.24, f32[]{:T(128)} %constant.43.clone.1), kind=kCustom, calls=%fused_computation.48 | custom fusion | flops 1575936 | bytes 2101760 | tf_op jit(solution)/shard_map/scatter-add | solution.py:73
  126.0 0.0 all-gather.5.cloned.1.call-start
  126.0 21.7 scatter_custom_fusion.1
  147.8 16.7 scatter_custom_fusion.3
  164.5 69.2 %all-reduce.4 = (f32[1024]{0:T(1024)S(1)}, f32[2048]{0:T(1024)S(1)}) all-reduce(f32[1024]{0:T(1024)S(1)} %scatter_custom_fusion.1, f32[2048]{0:T(1024)S(1)} %scatter_custom_fusion.3), channel_id=3, replica_groups=mesh['tile'=4,'block'=32] {'tile','block'}, use_global_device_ids=true, to_apply=%region_3.5.clone | all-reduce | flops 3072 | bytes 24576
  233.7 0.1 dynamic-slice_add_fusion.1
  233.7 47.5 %all-reduce.8.cloned.1.call-done = f32[1024,513]{1,0:T(8,128)} async-done(((f32[1024,513]{1,0:T(8,128)}), f32[1024,513]{1,0:T(8,128)}) %all-reduce.8.cloned.1.call-update) | async-done | bytes 2101264
  281.2 1.4 dynamic-slice_divide_fusion.1
  282.6 0.0 reduce-scatter.3.cloned.1.call-start
  282.7 67.0 %all-gather.5.cloned.1.call-done = f32[1024,513]{1,0:T(8,128)} async-done(((f32[8,513]{1,0:T(8,128)}), f32[1024,513]{1,0:T(8,128)}) %all-gather.5.cloned.1.call-update) | async-done | bytes 2101264 | tf_op jit(solution)/shard_map/all_gather | solution.py:32
  349.7 16.1 gather_fusion.3
  365.8 8.5 copy.25
  374.3 9.5 fusion.5
  383.8 8.2 copy.26
  392.0 23.6 %scatter_custom_fusion.2 = f32[2048,513]{1,0:T(8,128)} fusion(s32[3072]{0:T(1024)S(1)} %get-tuple-element.12, f32[3072,513]{1,0:T(8,128)} %copy.26, f32[]{:T(128)} %constant.43.clone.1), kind=kCustom, calls=%fused_computation.36 | custom fusion | flops 1575936 | bytes 4203008 | tf_op jit(solution)/shard_map/scatter-add | solution.py:76
  415.7 0.1 dynamic-slice_add_fusion
  415.7 635.6 %reduce-scatter.3.cloned.1.call-done = f32[16,513]{1,0:T(8,128)} async-done(((f32[2048,513]{1,0:T(8,128)}), f32[16,513]{1,0:T(8,128)}) %reduce-scatter.3.cloned.1.call-update) | async-done | bytes 32848 | tf_op jit(solution)/shard_map/reduce_scatter | solution.py:38
  1051.4 1.5 broadcast_divide_fusion.1
  1052.9 70.3 %all-gather.7.cloned.1.call-done = f32[2048,513]{1,0:T(8,128)} async-done(((f32[16,513]{1,0:T(8,128)}), f32[2048,513]{1,0:T(8,128)}) %all-gather.7.cloned.1.call-update) | async-done | bytes 4202512 | tf_op jit(solution)/shard_map/all_gather | solution.py:42
  1123.3 17.1 gather_fusion.4
  1140.4 8.5 copy.27
  1148.9 9.5 fusion.4
  1158.3 8.2 copy.28
  1166.6 22.5 %scatter_custom_fusion.4 = f32[1024,513]{1,0:T(8,128)} fusion(s32[3072]{0:T(1024)S(1)} %get-tuple-element.8, f32[3072,513]{1,0:T(8,128)} %copy.28, f32[]{:T(128)} %constant.43.clone.1), kind=kCustom, calls=%fused_computation.46 | custom fusion | flops 1575936 | bytes 2101760 | tf_op jit(solution)/shard_map/scatter-add | solution.py:73
  1189.2 149.1 %all-reduce.10.cloned.1.call-done = f32[1024,513]{1,0:T(8,128)} async-done(((f32[1024,513]{1,0:T(8,128)}), f32[1024,513]{1,0:T(8,128)}) %all-reduce.10.cloned.1.call-update) | async-done | bytes 2101264
  1338.2 1.4 dynamic-slice_divide_fusion
  1339.7 66.8 %all-gather.9.cloned.1.call-done = f32[1024,513]{1,0:T(8,128)} async-done(((f32[8,513]{1,0:T(8,128)}), f32[1024,513]{1,0:T(8,128)}) %all-gather.9.cloned.1.call-update) | async-done | bytes 2101264 | tf_op jit(solution)/shard_map/all_gather | solution.py:32
  1406.6 16.1 gather_fusion.5
  1422.7 8.5 copy.29
  1431.2 9.4 multiply_subtract_fusion
  1440.6 8.2 copy.30
  1448.8 23.7 %scatter_custom_fusion.5 = f32[2048,513]{1,0:T(8,128)} fusion(s32[3072]{0:T(1024)S(1)} %get-tuple-element.12, f32[3072,513]{1,0:T(8,128)} %copy.30, f32[]{:T(128)} %constant.43.clone.1), kind=kCustom, calls=%fused_computation.34 | custom fusion | flops 1575936 | bytes 4203008 | tf_op jit(solution)/shard_map/scatter-add | solution.py:76
  1472.6 635.7 %reduce-scatter.5.cloned.1.call-done = f32[16,513]{1,0:T(8,128)} async-done(((f32[2048,513]{1,0:T(8,128)}), f32[16,513]{1,0:T(8,128)}) %reduce-scatter.5.cloned.1.call-update) | async-done | bytes 32848 | tf_op jit(solution)/shard_map/reduce_scatter | solution.py:38
  2108.3 1.5 broadcast_divide_fusion
  2109.8 70.5 %all-gather.11.cloned.1.call-done = f32[2048,513]{1,0:T(8,128)} async-done(((f32[16,513]{1,0:T(8,128)}), f32[2048,513]{1,0:T(8,128)}) %all-gather.11.cloned.1.call-update) | async-done | bytes 4202512 | tf_op jit(solution)/shard_map/all_gather | solution.py:42
  2180.4 16.9 gather_fusion.6
  2197.3 8.5 copy.31
  2205.8 12.1 fusion.3
  (31 shorter events, 0.5 us)
Async XLA Ops:
  7.2 25.0 %copy-start = (s32[2048]{0:T(1024)S(1)}, s32[2048]{0:T(1024)}, u32[]{:S(2)}) copy-start(s32[2048]{0:T(1024)} %param.14) | copy-start | bytes 24580
  7.2 12.2 copy-start.2
  7.2 274.0 %all-reduce.8.cloned.1.call-start = ((), (), s32[]{:S(2)}) async-start(), calls=%async_computation.8 | async-start | bytes 5242880
  18.0 14.0 copy-start.4
  18.0 14.1 copy-start.5
  77.7 11.3 copy-start.3
  126.0 223.7 %all-gather.5.cloned.1.call-start = ((), (), s32[]{:S(2)}) async-start(), calls=%async_computation.2 | async-start | bytes 2641920 | tf_op jit(solution)/shard_map/all_gather | solution.py:32
  282.6 768.8 %reduce-scatter.3.cloned.1.call-start = ((), (), s32[]{:S(2)}) async-start(), calls=%async_computation.3 | async-start | bytes 5283840 | tf_op jit(solution)/shard_map/reduce_scatter | solution.py:38
  415.6 707.7 %all-gather.7.cloned.1.call-start = ((), (), s32[]{:S(2)}) async-start(), calls=%async_computation.4 | async-start | bytes 5283840 | tf_op jit(solution)/shard_map/all_gather | solution.py:42
  1052.9 285.3 %all-reduce.10.cloned.1.call-start = ((), (), s32[]{:S(2)}) async-start(), calls=%async_computation.9 | async-start | bytes 5242880
  1189.1 217.4 %all-gather.9.cloned.1.call-start = ((), (), s32[]{:S(2)}) async-start(), calls=%async_computation.5 | async-start | bytes 2641920 | tf_op jit(solution)/shard_map/all_gather | solution.py:32
  1339.7 768.7 %reduce-scatter.5.cloned.1.call-start = ((), (), s32[]{:S(2)}) async-start(), calls=%async_computation.6 | async-start | bytes 5283840 | tf_op jit(solution)/shard_map/reduce_scatter | solution.py:38
  1472.6 707.8 %all-gather.11.cloned.1.call-start = ((), (), s32[]{:S(2)}) async-start(), calls=%async_computation.7 | async-start | bytes 5283840 | tf_op jit(solution)/shard_map/all_gather | solution.py:42
  2205.8 12.1 copy-start.1
Sparse Core Ops, SparseCore 0:
  126.1 155.0 all-reduce.7
  285.4 64.2 all-gather.4
  415.7 635.6 reduce-scatter.2
  1054.8 68.4 all-gather.6
  1189.3 148.9 all-reduce.9
  1342.3 64.2 all-gather.8
  1472.7 635.6 reduce-scatter.4
  2111.9 68.4 all-gather.10
where the time goes:
time: 2230 us
  waiting for transfers between devices  1740 us (78%)
  other arithmetic  195 us (9%)
  local copies, waits for them, and re-layouts  191 us (9%)
  blocking collectives  69.2 us (3%)
    reduce_scatter x2, waiting for transfers between devices, settle_receivers(): lax.psum_scatter(partial_value, ('tile', 'block'), scatter_dimension=0, t...  1270 us
    unnamed x10, waiting for transfers between devices  197 us
    all_gather x2, waiting for transfers between devices, settle_receivers(): whole = lax.all_gather(mine, ('tile', 'block'), axis=0, tiled=True)  141 us
    all_gather x2, waiting for transfers between devices, settle_shots(): whole = lax.all_gather(mine, ('tile', 'block'), axis=0, tiled=True)  134 us
    unnamed x1, blocking collectives  69.2 us
    gather x4, local copies, waits for them, and re-layouts, shards(): resid = weighted - alive[:, None] * jnp.take(recv_whole, recv_row, axis=0)  51 us
    gather x4, local copies, waits for them, and re-layouts, shards(): resid = weighted - alive[:, None] * jnp.take(shot_whole, shot_row, axis=0)  49.3 us
    scatter-add x2, other arithmetic, shards(): partial_value = jax.ops.segment_sum(resid, recv_row, num_segments=nrecv)  47.3 us
  transfers between devices with their start and end apart: 8, of which 8 were waited for; matrix products, arithmetic and copies ran while one was open for 2% of the time, Pallas kernels for 0%

commit v1 on v0

v1 whole, which is shorter than its diff:
```python
import functools
import math

import jax
import jax.numpy as jnp
import ml_dtypes
import numpy as np
from jax import lax
from jax.experimental import pallas as pl
from jax.experimental.pallas import tpu as pltpu
from jax.sharding import PartitionSpec as P

FLOOR = 0.05
DAMP = 1.0

GROUPS = 32
SHOT = 32
RECV = 64
REACH = 3
MSG = SHOT + RECV + 8
SMSG = SHOT + 8
RMSG = RECV + 8
TILE = 512
MESH = pl.DeviceIdType.MESH
F32 = jnp.float32
BF16 = jnp.bfloat16
HIGH = lax.Precision.HIGHEST
NT = (((1,), (1,)), ((), ()))


def basis_table(nsamp):
    half = nsamp // 2
    freq = np.arange(half + 1, dtype=np.int64)
    sample = np.arange(nsamp, dtype=np.int64)
    phase = sample[:, None] * freq[None, :] % nsamp
    angle = phase.astype(np.float32) * np.float32(2.0 * math.pi / nsamp)
    norm = np.float32(1.0 / math.sqrt(nsamp))
    cos = (np.cos(angle) * norm).astype(ml_dtypes.bfloat16)
    sin = (-np.sin(angle) * norm).astype(ml_dtypes.bfloat16)
    odd = float(sin[1, half])
    sine = sin[:, :half].copy()
    sine[:, 0] = cos[:, half]
    parts = []
    for k in range(0, half, 128):
        parts += [cos[:, k : k + 128], sine[:, k : k + 128]]
    return np.concatenate(parts, axis=1), odd


def place():
    d = lax.axis_index("tile") * 32 + lax.axis_index("block")
    return d, d // 64, (d % 64) // 2, d % 2


def device(side, group, core):
    return side * 64 + 2 * lax.rem(group + GROUPS, GROUPS) + core


def coords(d):
    return (d // 32, lax.rem(d, 32))


def local_rows(ident, live, group, core, owned):
    half = owned // 2
    total = half * GROUPS
    side = ident // total
    within = ident & (total - 1)
    j = (within // half - (group - 2 + core) + 2 * GROUPS) & (GROUPS - 1)
    row = side * half + (within & (half - 1))
    return jnp.where(live, j, -1), row


def split(x):
    hi = x.astype(BF16)
    return hi, (x - hi.astype(F32)).astype(BF16)


def solve_kernel(
    odd, shot_ref, recv_ref, count_ref, samples, basis, spec_out, table,
    x, b, w, spec, acc, cacc, racc, msgs, cmsg, inbox, cin, cg, csr, crs,
    s1, r1, s2, r2, in_sem, b_sem, out_sem, c_send, c_recv, g_send, g_recv,
    p_send, p_recv, s1_send, s1_recv, r1_send, r1_recv, s2_send, s2_recv,
    ts_send, ts_recv, tr_send, tr_recv,
):
    me, side, group, core = place()
    s = 2 * side + core
    rows = x.shape[0]
    tiles = rows // TILE

    def member(st, g):
        return device(st // 2, g, lax.rem(st, 2))

    def window_peer(n):
        j, st = n // 4, lax.rem(n, 4)
        return member(st, group + 2 - lax.rem(st, 2) - j)

    def remote(src, dst, send, recv, target):
        return pltpu.make_async_remote_copy(
            src_ref=src, dst_ref=dst, send_sem=send, recv_sem=recv,
            device_id=coords(target), device_id_type=MESH,
        )

    barrier = pltpu.get_barrier_semaphore()

    def greet(n, _):
        off, st = n // 4 - 2, lax.rem(n, 4)
        other = member(st, group + off)

        @pl.when(other != me)
        def _():
            pl.semaphore_signal(barrier, inc=1, device_id=coords(other), device_id_type=MESH)

        return 0

    lax.fori_loop(0, 20, greet, 0)
    for off in (-REACH, REACH):
        pl.semaphore_signal(
            barrier, inc=1, device_id=coords(member(s, group + off)), device_id_type=MESH
        )

    def load(i):
        part = pl.ds(pl.multiple_of(i * TILE, TILE), TILE)
        return pltpu.make_async_copy(samples.at[part], x.at[part], in_sem.at[i])

    def load_basis(k):
        part = pl.ds(256 * k, 256)
        return pltpu.make_async_copy(basis.at[:, part], b.at[:, part], b_sem.at[k])

    load_basis(0).start()
    for i in range(tiles):
        load(i).start()
    for k in range(1, 4):
        load_basis(k).start()

    slot = lax.broadcasted_iota(jnp.int32, (1, rows), 1)
    live = slot < count_ref[0]
    sj, srow = local_rows(shot_ref[...], live, group, core, SHOT)
    rj, rrow = local_rows(recv_ref[...], live, group, core, RECV)
    srow = jnp.where(live, sj * SHOT + srow, -1)
    rrow = jnp.where(live, rj * RECV + rrow, -1)
    for i in range(tiles):
        cols = slice(i * TILE, (i + 1) * TILE)
        ident = lax.broadcasted_iota(jnp.int32, (4 * SHOT, TILE), 0)
        w[: 4 * SHOT, cols] = (ident == srow[:, cols]).astype(F32).astype(BF16)
        ident = lax.broadcasted_iota(jnp.int32, (4 * RECV, TILE), 0)
        w[4 * SHOT :, cols] = (ident == rrow[:, cols]).astype(F32).astype(BF16)
    cacc[...] = jnp.zeros_like(cacc)
    racc[...] = jnp.zeros_like(racc)

    def tally(i, _):
        part = pl.ds(pl.multiple_of(i * TILE, TILE), TILE)
        ws, wr = w[: 4 * SHOT, part], w[4 * SHOT :, part]
        cacc[...] += lax.dot_general(ws, wr, NT, preferred_element_type=F32)
        racc[...] += lax.dot_general(wr, ws, NT, preferred_element_type=F32)
        return 0

    lax.fori_loop(0, tiles, tally, 0)
    for j in range(4):
        for st in range(4):
            top = j * SHOT + 8 * st
            cmsg[j, st, 0:8] = cacc[top : top + 8, 0:128]
            cmsg[j, st, 8:16] = cacc[top : top + 8, 128:256]
            top = j * RECV + 16 * st
            cmsg[j, st, 16:32] = racc[top : top + 16, :]
    csr[...] = jnp.zeros_like(csr)
    crs[...] = jnp.zeros_like(crs)
    pl.semaphore_wait(barrier, 21)

    def count_copy(n):
        j, st = n // 4, lax.rem(n, 4)
        target = member(st, group - 2 + core + j)
        return target, remote(
            cmsg.at[j, st], cin.at[4 * j + s], c_send.at[n], c_recv.at[4 * j + s], target
        )

    def send_count(n, _):
        target, copy = count_copy(n)

        @pl.when(target != me)
        def _():
            copy.start()

        return 0

    lax.fori_loop(0, 16, send_count, 0)
    cin[4 * (2 - core) + s] = cmsg[2 - core, s]

    lane = lax.broadcasted_iota(jnp.int32, (TILE, 128), 1)
    lane8 = lax.broadcasted_iota(jnp.int32, (8, 128), 1)

    def log_spectra(k):
        load_basis(k).wait()
        acc[...] = jnp.zeros_like(acc)

        def step(i, _):
            if k == 0:
                load(i).wait()
            part = pl.ds(pl.multiple_of(i * TILE, TILE), TILE)
            y = jnp.dot(x[part], b[:, 256 * k : 256 * k + 256], preferred_element_type=F32)
            re, im = y[:, :128], y[:, 128:]
            power = im * im
            if k == 0:
                power = jnp.where(lane == 0, 0.0, power)
            value = jnp.log(re * re + power + FLOOR)
            spec[k, part] = value
            pieces = list(split(value))
            if k == 0:
                re0, re512 = re[:, 0:1], im[:, 0:1]
                im512 = (odd * 16.0) * (re0 - re512)
                power = jnp.broadcast_to(re512 * re512 + im512 * im512, (TILE, 128))
                value = jnp.log(power + FLOOR)
                spec[4, part] = value
                hi, lo = split(value)
                pieces.append(jnp.where(lane == 0, hi.astype(F32), lo.astype(F32)).astype(BF16))
            width = 128 * len(pieces)
            acc[:, :width] += jnp.dot(
                w[:, part], jnp.concatenate(pieces, axis=1), preferred_element_type=F32
            )
            return 0

        lax.fori_loop(0, tiles, step, 0)
        pltpu.make_async_copy(spec.at[k], spec_out.at[k], out_sem.at[k]).start()
        for j in range(4):
            for first, size, to in ((j * SHOT, SHOT, 0), (4 * SHOT + j * RECV, RECV, SHOT)):
                msgs[k, j, to : to + size] = (
                    acc[first : first + size, 0:128] + acc[first : first + size, 128:256]
                )
        if k == 0:
            pltpu.make_async_copy(spec.at[4], spec_out.at[4], out_sem.at[4]).start()
            both = acc[:, 256:384]
            both = both + pltpu.roll(both, 127, 1)
            line = [
                jnp.broadcast_to(jnp.transpose(both[128 * v : 128 * v + 128])[0:1], (8, 128))
                for v in range(3)
            ]
            for j in range(4):
                shots = pltpu.roll(line[0], (128 - SHOT * j) % 128, 1)
                recvs = pltpu.roll(line[1 + j // 2], (SHOT + 128 - RECV * (j % 2)) % 128, 1)
                nyquist = jnp.where(lane8 < SHOT, shots, recvs)
                nyquist = jnp.where(lane8 < SHOT + RECV, nyquist, 0.0)
                for kk in range(4):
                    msgs[kk, j, SHOT + RECV : MSG] = nyquist

    def sum_copy(k, j):
        target = member(k, group - 2 + core + j)
        return target, remote(
            msgs.at[k, j], inbox.at[4 * j + s], p_send.at[4 * k + j], p_recv.at[4 * j + s], target
        )

    def send_sums(k):
        for j in range(4):
            target, copy = sum_copy(k, j)

            @pl.when(target != me)
            def _():
                copy.start()

        @pl.when(s == k)
        def _():
            inbox[4 * (2 - core) + k] = msgs[k, 2 - core]

    def arrived(buf, send, recv):
        def one(n, _):
            source = window_peer(n)

            @pl.when(source != me)
            def _():
                remote(buf.at[n], buf.at[n], send.at[n], recv.at[n], source).wait_recv()

            return 0

        lax.fori_loop(0, 16, one, 0)

    def member_copy(st):
        return remote(cg.at[s], cg.at[s], g_send.at[st], g_recv.at[s], member(st, group))

    def share_counts():
        arrived(cin, c_send, c_recv)
        shots = jnp.zeros((8, 512), F32)
        recvs = jnp.zeros((16, 256), F32)
        for j in range(4):
            part = cin[4 * j] + cin[4 * j + 1] + cin[4 * j + 2] + cin[4 * j + 3]
            wide = jnp.concatenate([part[0:8], part[8:16], jnp.zeros((8, 256), F32)], axis=1)
            shots += pltpu.roll(wide, RECV * (3 - j), 1) if j < 3 else wide
            wide = jnp.concatenate([part[16:32], jnp.zeros((16, 128), F32)], axis=1)
            recvs += pltpu.roll(wide, SHOT * (3 - j), 1) if j < 3 else wide
        for v in range(4):
            cg[s, 8 * v : 8 * v + 8] = shots[:, 128 * v : 128 * v + 128]
        for v in range(2):
            cg[s, 32 + 16 * v : 48 + 16 * v] = recvs[:, 128 * v : 128 * v + 128]
        for st in range(4):

            @pl.when(st != s)
            def _():
                member_copy(st).start()

    def take_counts():
        for st in range(4):

            @pl.when(st != s)
            def _():
                remote(
                    cg.at[st], cg.at[st], g_send.at[st], g_recv.at[st], member(st, group)
                ).wait_recv()

        for st in range(4):
            for v in range(4):
                csr[8 * st : 8 * st + 8, 128 * v : 128 * v + 128] = cg[st, 8 * v : 8 * v + 8]
            for v in range(2):
                crs[16 * st : 16 * st + 16, 128 * v : 128 * v + 128] = cg[
                    st, 32 + 16 * v : 48 + 16 * v
                ]

    log_spectra(0)
    send_sums(0)
    log_spectra(1)
    send_sums(1)
    share_counts()
    log_spectra(2)
    send_sums(2)
    take_counts()
    log_spectra(3)
    send_sums(3)

    shot_counts = jnp.sum(csr[0:SHOT], axis=1, keepdims=True) + DAMP
    recv_counts = jnp.sum(crs[0:RECV], axis=1, keepdims=True) + DAMP

    def matmul(p, q):
        return jnp.dot(p, q, precision=HIGH, preferred_element_type=F32)

    def matmul_nt(p, q):
        return lax.dot_general(p, q, NT, precision=HIGH, preferred_element_type=F32)

    shot_line = matmul_nt(jnp.ones((8, 512), F32), csr[...]) + DAMP
    recv_line = matmul_nt(jnp.ones((8, 256), F32), crs[...]) + DAMP
    for buf, size in ((s1, SMSG), (r1, RMSG), (s2, SMSG)):
        buf[7] = jnp.zeros((size, 128), F32)

    arrived(inbox, p_send, p_recv)
    total = inbox[0]
    for n in range(1, 16):
        total = total + inbox[n]
    shot_sum = total[0:SHOT]
    recv_sum = total[SHOT : SHOT + RECV]
    ends = total[SHOT + RECV : MSG]
    shot_end = jnp.where(lane8 < SHOT, ends, 0.0)
    recv_end = jnp.where(lane8 < RECV, pltpu.roll(ends, 128 - SHOT, 1), 0.0)

    def spread_copy(buf, send, recv, off):
        return remote(
            buf.at[3], buf.at[3 - off], send.at[3 - off], recv.at[3 - off], member(s, group + off)
        )

    offsets = [off for off in (3, -3, 2, -2, 1, -1)]

    def spread(buf, send, recv):
        for off in offsets:
            spread_copy(buf, send, recv, off).start()

    def gathered(buf, send, recv):
        for off in offsets:
            spread_copy(buf, send, recv, off).wait_recv()

    def shot_matrix(buf):
        main = buf[:, 0:SHOT].reshape(8 * SHOT, 128)
        line = [jnp.zeros((8, 128), F32) for _ in range(2)]
        for n in range(7):
            piece = buf[n, SHOT:SMSG]
            line[n // 4] += pltpu.roll(piece, SHOT * (n % 4), 1) if n % 4 else piece
        return main, jnp.concatenate(line, axis=1)

    def recv_matrix(buf):
        main = buf[:, 0:RECV].reshape(8 * RECV, 128)
        line = [jnp.zeros((8, 128), F32) for _ in range(4)]
        for n in range(7):
            piece = buf[n, RECV:RMSG]
            line[n // 2] += pltpu.roll(piece, RECV, 1) if n % 2 else piece
        return main, jnp.concatenate(line, axis=1)

    s1[3, 0:SHOT] = shot_sum / shot_counts
    s1[3, SHOT:SMSG] = shot_end / shot_line
    spread(s1, s1_send, s1_recv)
    gathered(s1, s1_send, s1_recv)

    main, line = shot_matrix(s1)
    r1[3, 0:RECV] = (recv_sum - matmul(crs[0:RECV], main)) / recv_counts
    r1[3, RECV:RMSG] = (recv_end - matmul_nt(line, crs[...])) / recv_line
    spread(r1, r1_send, r1_recv)
    gathered(r1, r1_send, r1_recv)

    main, line = recv_matrix(r1)
    s2[3, 0:SHOT] = (shot_sum - matmul(csr[0:SHOT], main)) / shot_counts
    s2[3, SHOT:SMSG] = (shot_end - matmul_nt(line, csr[...])) / shot_line
    spread(s2, s2_send, s2_recv)

    def table_copy(src, first, size, send, recv, n):
        j = n // 4
        return remote(
            src, table.at[s, j, pl.ds(first, size)], send.at[n], recv.at[4 * s + j], window_peer(n)
        )

    def publish(src, first, size, send, recv):
        def one(n, _):
            @pl.when(window_peer(n) != me)
            def _():
                table_copy(src, first, size, send, recv, n).start()

            return 0

        lax.fori_loop(0, 16, one, 0)

    publish(s2.at[3], 0, SMSG, ts_send, ts_recv)
    table[s, 2 - core, 0:SMSG] = s2[3]
    gathered(s2, s2_send, s2_recv)

    main, line = shot_matrix(s2)
    r2[0:RECV] = (recv_sum - matmul(crs[0:RECV], main)) / recv_counts
    r2[RECV:RMSG] = (recv_end - matmul_nt(line, crs[...])) / recv_line
    publish(r2, SMSG, RMSG, tr_send, tr_recv)
    table[s, 2 - core, SMSG : SMSG + RMSG] = r2[...]

    def drain(n, _):
        target, copy = count_copy(n)

        @pl.when(target != me)
        def _():
            copy.wait_send()

        @pl.when(window_peer(n) != me)
        def _():
            table_copy(s2.at[3], 0, SMSG, ts_send, ts_recv, n).wait_send()
            table_copy(r2, SMSG, RMSG, tr_send, tr_recv, n).wait_send()

        st, j = n // 4, lax.rem(n, 4)
        source = member(st, group - 2 + core + j)

        @pl.when(source != me)
        def _():
            for src, first, size, send, recv in (
                (s2.at[3], 0, SMSG, ts_send, ts_recv),
                (r2, SMSG, RMSG, tr_send, tr_recv),
            ):
                remote(
                    src, table.at[st, j, pl.ds(first, size)], send.at[n], recv.at[n], source
                ).wait_recv()

        return 0

    lax.fori_loop(0, 16, drain, 0)
    for k in range(4):
        for j in range(4):
            target, copy = sum_copy(k, j)

            @pl.when(target != me)
            def _():
                copy.wait_send()

        @pl.when(k != s)
        def _():
            member_copy(k).wait_send()

    for off in offsets:
        spread_copy(s1, s1_send, s1_recv, off).wait_send()
        spread_copy(r1, r1_send, r1_recv, off).wait_send()
        spread_copy(s2, s2_send, s2_recv, off).wait_send()
    for k in range(5):
        pltpu.make_async_copy(spec.at[k], spec_out.at[k], out_sem.at[k]).wait()


def solve(basis, odd, shot_id, recv_id, counts, samples):
    rows, nsamp = samples.shape
    dma = pltpu.SemaphoreType.DMA
    vmem = pl.BlockSpec(memory_space=pltpu.VMEM)
    hbm = pl.BlockSpec(memory_space=pl.ANY)
    return pl.pallas_call(
        functools.partial(solve_kernel, odd),
        out_shape=(
            jax.ShapeDtypeStruct((5, rows, 128), F32),
            jax.ShapeDtypeStruct((4, 4, SMSG + RMSG, 128), F32),
        ),
        in_specs=[vmem, vmem, pl.BlockSpec(memory_space=pltpu.SMEM), hbm, hbm],
        out_specs=(hbm, vmem),
        scratch_shapes=[
            pltpu.VMEM((rows, nsamp), BF16),
            pltpu.VMEM((nsamp, nsamp), BF16),
            pltpu.VMEM((4 * (SHOT + RECV), rows), BF16),
            pltpu.VMEM((5, rows, 128), F32),
            pltpu.VMEM((4 * (SHOT + RECV), 384), F32),
            pltpu.VMEM((4 * SHOT, 4 * RECV), F32),
            pltpu.VMEM((4 * RECV, 4 * SHOT), F32),
            pltpu.VMEM((4, 4, MSG, 128), F32),
            pltpu.VMEM((4, 4, 32, 128), F32),
            pltpu.VMEM((16, MSG, 128), F32),
            pltpu.VMEM((16, 32, 128), F32),
            pltpu.VMEM((4, 64, 128), F32),
            pltpu.VMEM((128, 8 * RECV), F32),
            pltpu.VMEM((128, 8 * SHOT), F32),
            pltpu.VMEM((8, SMSG, 128), F32),
            pltpu.VMEM((8, RMSG, 128), F32),
            pltpu.VMEM((8, SMSG, 128), F32),
            pltpu.VMEM((RMSG, 128), F32),
            dma((rows // TILE,)),
            dma((4,)),
            dma((5,)),
            dma((16,)), dma((16,)),
            dma((4,)), dma((4,)),
            dma((16,)), dma((16,)),
            dma((7,)), dma((7,)),
            dma((7,)), dma((7,)),
            dma((7,)), dma((7,)),
            dma((16,)), dma((16,)),
            dma((16,)), dma((16,)),
        ],
        compiler_params=pltpu.CompilerParams(
            collective_id=0, has_side_effects=True, vmem_limit_bytes=40 * 2**20
        ),
        cost_estimate=pl.CostEstimate(
            flops=9 * 10**9, bytes_accessed=16 * 10**6, transcendentals=2 * 10**6
        ),
    )(shot_id, recv_id, counts, samples, basis)


def residual_kernel(
    shot_ref, recv_ref, count_ref, shot_owner, recv_owner, spec, table, out, shot_out, recv_out, t
):
    step = pl.program_id(0)
    d, side, group, core = place()
    s = 2 * side + core
    size = SHOT + RECV
    half = 4 * size

    @pl.when(step == 0)
    def _():
        lane = lax.broadcasted_iota(jnp.int32, (8, 128), 1)
        lines = []
        for j in range(4):
            shots = table[0, j, SHOT:SMSG]
            recvs = pltpu.roll(table[0, j, SMSG + RECV : SMSG + RMSG], SHOT, 1)
            lines.append(jnp.where(lane < SHOT, shots, recvs)[0:1])
        lines.append(jnp.zeros((124, 128), F32))
        turned = jnp.transpose(jnp.concatenate(lines, axis=0))
        for j in range(4):
            for k in range(5):
                if k < 4:
                    value = jnp.concatenate(
                        [table[k, j, 0:SHOT], table[k, j, SMSG : SMSG + RECV]], axis=0
                    )
                else:
                    value = (pltpu.roll(turned, 128 - j, 1) if j else turned)[0:size]
                hi, lo = split(value)
                t[size * j : size * j + size, 128 * k : 128 * k + 128] = hi
                t[half + size * j : half + size * j + size, 128 * k : 128 * k + 128] = lo

        j = 2 - core
        ends_s = jnp.transpose(
            jnp.concatenate([table[0, j, SHOT:SMSG], jnp.zeros((120, 128), F32)], axis=0)
        )
        ends_r = jnp.transpose(
            jnp.concatenate([table[0, j, SMSG + RECV : SMSG + RMSG], jnp.zeros((120, 128), F32)], axis=0)
        )
        for owner, owned, first, ends, dst in (
            (shot_owner, 8, 0, ends_s, shot_out),
            (recv_owner, 16, SMSG, ends_r, recv_out),
        ):
            top = pl.multiple_of(first + owned * s, 8)
            index = lax.broadcasted_iota(jnp.int32, (owned, 1), 0)
            pieces = [table[k, j, pl.ds(top, owned)] for k in range(4)]
            end = jnp.zeros((owned, 128), F32)
            for st in range(4):
                end = jnp.where(s == st, ends[owned * st : owned * st + owned], end)
            pieces.append(end)
            for k in range(5):
                value = jnp.zeros((owned, 128), F32)
                for i in range(owned):
                    row = owner[owned * d + i] - owned * d
                    value = jnp.where(index == row, pieces[k][i : i + 1], value)
                if k < 4:
                    dst[:, 128 * k : 128 * k + 128] = value
                else:
                    dst[:, 512:513] = value[:, 0:1]

    rows = out.shape[0]
    count = count_ref[0] - step * rows

    def turned(ref, owned, to):
        live = lax.broadcasted_iota(jnp.int32, (1, rows), 1) < count
        j, row = local_rows(ref[...], live, group, core, owned)
        row = jnp.where(live, j * size + to + row, -1)
        return jnp.transpose(jnp.broadcast_to(row, (128, rows)))

    shots, recvs = turned(shot_ref, SHOT, 0), turned(recv_ref, RECV, SHOT)
    lane = lax.broadcasted_iota(jnp.int32, (rows, 128), 1)
    hot = [
        ((shots == lane + 128 * v) | (recvs == lane + 128 * v)).astype(F32).astype(BF16)
        for v in range(3)
    ]
    both = jnp.concatenate(hot + hot, axis=1)
    terms = jnp.dot(both, t[...], preferred_element_type=F32)
    live = lax.broadcasted_iota(jnp.int32, (rows, 128), 0) < count
    for k in range(4):
        part = slice(128 * k, 128 * k + 128)
        out[:, part] = jnp.where(live, spec[k], 0.0) - terms[:, part]
    out[:, 512:513] = (jnp.where(live, spec[4], 0.0) - terms[:, 512:640])[:, 0:1]


def residuals(shot_id, recv_id, counts, shot_owner, recv_owner, spec, table):
    rows = spec.shape[1]
    smem = pl.BlockSpec(memory_space=pltpu.SMEM)
    return pl.pallas_call(
        residual_kernel,
        grid=(rows // TILE,),
        out_shape=(
            jax.ShapeDtypeStruct((rows, 513), F32),
            jax.ShapeDtypeStruct((8, 513), F32),
            jax.ShapeDtypeStruct((16, 513), F32),
        ),
        in_specs=[
            pl.BlockSpec((1, TILE), lambda i: (0, i)),
            pl.BlockSpec((1, TILE), lambda i: (0, i)),
            smem,
            smem,
            smem,
            pl.BlockSpec((5, TILE, 128), lambda i: (0, i, 0)),
            pl.BlockSpec((4, 4, SMSG + RMSG, 128), lambda i: (0, 0, 0, 0)),
        ],
        out_specs=(
            pl.BlockSpec((TILE, 513), lambda i: (i, 0)),
            pl.BlockSpec((8, 513), lambda i: (0, 0)),
            pl.BlockSpec((16, 513), lambda i: (0, 0)),
        ),
        scratch_shapes=[pltpu.VMEM((8 * (SHOT + RECV), 640), BF16)],
        compiler_params=pltpu.CompilerParams(vmem_limit_bytes=32 * 2**20),
        cost_estimate=pl.CostEstimate(
            flops=3 * 10**9, bytes_accessed=16 * 10**6, transcendentals=0
        ),
    )(shot_id, recv_id, counts, shot_owner, recv_owner, spec, table)


def shards(basis, odd, samples, shot_id, recv_id, shot_owner, recv_owner, counts):
    rows = samples.shape[0]
    shot_id, recv_id = shot_id.reshape(1, rows), recv_id.reshape(1, rows)
    spec, table = solve(basis, odd, shot_id, recv_id, counts, samples)
    residual, shots, recvs = residuals(
        shot_id, recv_id, counts, shot_owner, recv_owner, spec, table
    )
    return shots, recvs, residual


def solution(mesh):
    basis, odd = basis_table(1024)

    def run(*args):
        return shards(jnp.asarray(basis), odd, *args)

    return jax.shard_map(
        run,
        mesh=mesh,
        in_specs=(
            P(("tile", "block"), None),
            P(("tile", "block")),
            P(("tile", "block")),
            P(),
            P(),
            P(("tile", "block")),
        ),
        out_specs=(
            P(("tile", "block"), None),
            P(("tile", "block"), None),
            P(("tile", "block"), None),
        ),
        check_vma=False,
    )
```

time: 2230 us -> 100 us (0.04)
  the two profiles are of different devices: /device:TPU:1 before, /device:TPU:35 now
where the time goes in v1:
time: 100 us
  Pallas kernels  78.1 us (78%)
  local copies, waits for them, and re-layouts  20.6 us (21%)
  between operations  1.34 us (1%)
    pallas_call x1, Pallas kernels, solve(): pl.pallas_call(functools.partial(solve_kernel, odd), out_shape=(jax.Shape...  71 us
    unnamed x17, local copies, waits for them, and re-layouts  20.6 us
    pallas_call x1, Pallas kernels, residuals(): pl.pallas_call(residual_kernel, grid=(rows // TILE,), out_shape=(jax.Shap...  7.1 us

profile of v1, /device:TPU:35, one launch (start us, length us, event | category | flops | bytes accessed | tf_op | source)
XLA Modules:
  0.0 100.0 jit_solution(14441521562030586515)
XLA Ops:
  1.3 0.0 copy-start.1
  1.3 2.8 %copy-done.1 = bf16[3072,1024]{1,0:T(8,128)(2,1)S(1)} copy-done((bf16[3072,1024]{1,0:T(8,128)(2,1)S(1)}, bf16[3072,1024]{1,0:T(8,128)(2,1)}, u32[]{:S(2)}) %copy-start.1) | copy-done | bytes 6291480
  4.1 0.0 copy-start.2
  4.1 0.7 copy-done.2
  4.8 0.0 copy-start.3
  4.8 0.7 copy-done.3
  5.5 0.0 copy-start.6
  5.5 1.6 %copy-done.6 = bf16[1024,1024]{1,0:T(8,128)(2,1)S(1)} copy-done((bf16[1024,1024]{1,0:T(8,128)(2,1)S(1)}, bf16[1024,1024]{1,0:T(8,128)(2,1)}, u32[]{:S(2)}) %copy-start.6) | copy-done | bytes 2097176
  7.1 0.0 copy-start.4
  7.1 0.0 copy-start.5
  7.1 71.0 %shard_map.94 = (f32[5,3072,128]{2,1,0:T(8,128)}, f32[4,4,112,128]{3,2,1,0:T(8,128)S(1)}) custom-call(s32[1,3072]{1,0:T(1,128)S(1)} %bitcast.2, s32[1,3072]{1,0:T(1,128)S(1)} %bitcast.4, s32[1]{0:T(128)S(6)} %copy.11.count_ref, bf16[3072,1024]{1,0:T(8,128)(2,1)S(1)} %copy-done.1, bf16[1024,1024]{1,0:T(8,128)(2,1)S(1)} %copy-done.6), custom_call_target="tpu_custom_call" | custom-call | flops 8999999488 | bytes 16000000 | tf_op jit(solution)/shard_map/pallas_call | solution.py:474
  78.0 0.0 copy-done.4
  78.1 0.0 copy-done.5
  78.1 0.0 copy-start.7
  78.1 3.2 %copy-done.7 = f32[5,3072,128]{2,1,0:T(8,128)S(1)} copy-done((f32[5,3072,128]{2,1,0:T(8,128)S(1)}, f32[5,3072,128]{2,1,0:T(8,128)}, u32[]{:S(2)}) %copy-start.7) | copy-done | bytes 7864344
  81.3 7.1 %shard_map.95 = (f32[3072,513]{1,0:T(8,128)S(1)}, f32[8,513]{1,0:T(8,128)}, f32[16,513]{1,0:T(8,128)}) custom-call(s32[1,3072]{1,0:T(1,128)S(1)} %bitcast.3, s32[1,3072]{1,0:T(1,128)S(1)} %bitcast.5, s32[1]{0:T(128)S(6)} %copy.11.count_ref, s32[1024]{0:T(1024)S(1)} %copy-done.5, s32[2048]{0:T(1024)S(1)} %copy-done.4, f32[5,3072,128]{2,1,0:T(8,128)S(1)} %copy-done.7, ...), custom_call_target="tpu_custom_call" | custom-call | flops 3000000000 | bytes 16000000 | tf_op jit(solution)/shard_map/pallas_call | solution.py:608
  88.4 0.0 copy-start
  88.4 3.0 %copy-done = f32[3072,513]{1,0:T(8,128)} copy-done((f32[3072,513]{1,0:T(8,128)}, f32[3072,513]{1,0:T(8,128)S(1)}, u32[]{:S(2)}) %copy-start) | copy-done | bytes 6303768
  91.5 8.5 %copy.10 = f32[3072,513]{0,1:T(8,128)} copy(f32[3072,513]{1,0:T(8,128)} %copy-done) | data formatting | bytes 12607488
Async XLA Ops:
  1.3 2.8 %copy-start.1 = (bf16[3072,1024]{1,0:T(8,128)(2,1)S(1)}, bf16[3072,1024]{1,0:T(8,128)(2,1)}, u32[]{:S(2)}) copy-start(bf16[3072,1024]{1,0:T(8,128)(2,1)} %samples.1) | copy-start | bytes 18874372
  4.1 0.7 copy-start.2
  4.8 0.7 copy-start.3
  5.5 1.6 %copy-start.6 = (bf16[1024,1024]{1,0:T(8,128)(2,1)S(1)}, bf16[1024,1024]{1,0:T(8,128)(2,1)}, u32[]{:S(2)}) copy-start(bf16[1024,1024]{1,0:T(8,128)(2,1)} %constant.2.clone.basis) | copy-start | bytes 6291460
  7.1 71.0 %copy-start.4 = (s32[2048]{0:T(1024)S(1)}, s32[2048]{0:T(1024)}, u32[]{:S(2)}) copy-start(s32[2048]{0:T(1024)} %recv_owner.1) | copy-start | bytes 24580
  7.1 71.0 %copy-start.5 = (s32[1024]{0:T(1024)S(1)}, s32[1024]{0:T(1024)}, u32[]{:S(2)}) copy-start(s32[1024]{0:T(1024)} %shot_owner.1) | copy-start | bytes 12292
  78.1 3.2 %copy-start.7 = (f32[5,3072,128]{2,1,0:T(8,128)S(1)}, f32[5,3072,128]{2,1,0:T(8,128)}, u32[]{:S(2)}) copy-start(f32[5,3072,128]{2,1,0:T(8,128)} %get-tuple-element.8.spec) | copy-start | bytes 23592964
  88.4 3.1 %copy-start = (f32[3072,513]{1,0:T(8,128)}, f32[3072,513]{1,0:T(8,128)S(1)}, u32[]{:S(2)}) copy-start(f32[3072,513]{1,0:T(8,128)S(1)} %get-tuple-element.15) | copy-start | bytes 18911236

commit v2 on v1

v2 whole, which is shorter than its diff:
```python
import functools
import math

import jax
import jax.numpy as jnp
import ml_dtypes
import numpy as np
from jax import lax
from jax.experimental import pallas as pl
from jax.experimental.pallas import tpu as pltpu
from jax.sharding import PartitionSpec as P

FLOOR = 0.05
DAMP = 1.0

GROUPS = 32
SHOT = 32
RECV = 64
REACH = 3
MSG = SHOT + RECV + 8
SMSG = SHOT + 8
RMSG = RECV + 8
TILE = 1024
LANES = 512
MESH = pl.DeviceIdType.MESH
F32 = jnp.float32
BF16 = jnp.bfloat16
HIGH = lax.Precision.HIGHEST
NT = (((1,), (1,)), ((), ()))


def basis_table(nsamp):
    half = nsamp // 2
    freq = np.arange(half + 1, dtype=np.int64)
    sample = np.arange(nsamp, dtype=np.int64)
    phase = sample[:, None] * freq[None, :] % nsamp
    angle = phase.astype(np.float32) * np.float32(2.0 * math.pi / nsamp)
    norm = np.float32(1.0 / math.sqrt(nsamp))
    cos = (np.cos(angle) * norm).astype(ml_dtypes.bfloat16)
    sin = (-np.sin(angle) * norm).astype(ml_dtypes.bfloat16)
    odd = float(sin[1, half])
    parts = []
    for k in range(0, half, 128):
        parts += [cos[:, k : k + 128], sin[:, k : k + 128]]
    return np.concatenate(parts, axis=1), (odd, float(norm))


def place():
    d = lax.axis_index("tile") * 32 + lax.axis_index("block")
    return d, d // 64, (d % 64) // 2, d % 2


def device(side, group, core):
    return side * 64 + 2 * lax.rem(group + GROUPS, GROUPS) + core


def coords(d):
    return (d // 32, lax.rem(d, 32))


def local_rows(ident, live, group, core, owned):
    half = owned // 2
    total = half * GROUPS
    side = ident // total
    within = ident & (total - 1)
    j = (within // half - (group - 2 + core) + 2 * GROUPS) & (GROUPS - 1)
    row = side * half + (within & (half - 1))
    return jnp.where(live, j, -1), row


def split(x):
    hi = x.astype(BF16)
    return hi, (x - hi.astype(F32)).astype(BF16)


def solve_kernel(
    odd, shot_ref, recv_ref, count_ref, samples, basis, spec, w, table,
    x, b, shot_ids, recv_ids, acc, cacc, racc, msgs, cmsg, inbox, cin, cg, csr, crs,
    s1, r1, s2, r2, in_sem, b_sem, id_sem, c_send, c_recv, g_send, g_recv,
    p_send, p_recv, s1_send, s1_recv, r1_send, r1_recv, s2_send, s2_recv,
    ts_send, ts_recv, tr_send, tr_recv,
):
    me, side, group, core = place()
    s = 2 * side + core
    rows = x.shape[0]
    tiles = rows // TILE

    sides, cores = (side, 1 - side), (core, 1 - core)
    places = {}
    for off in range(-REACH, REACH + 1):
        g = lax.rem(group + (off + GROUPS), GROUPS)
        places[off] = (g // 16, 2 * lax.rem(g, 16))
    far_off = 4 * core - 2
    g = lax.rem(group + far_off + GROUPS, GROUPS)
    places["far"] = (g // 16, 2 * lax.rem(g, 16))

    def peer(off, r):
        tile, block = places[off]
        return (2 * sides[r // 2] + tile, block + cores[r % 2])

    def edge_peer(off, r1):
        tile, block = places[off]
        return (2 * sides[r1] + tile, block + (0 if off > 0 else 1))

    window = ((0, 2 - core), (-1, 1 - core), (1, 3 - core), ("far", 3 * core))

    def landing(off, r):
        if off == "far":
            return 12 + 2 * core + r // 2
        return {0: r, 1: 4 + r, -1: 8 + r}[off]

    def remote(src, dst, send, recv, target):
        return pltpu.make_async_remote_copy(
            src_ref=src, dst_ref=dst, send_sem=send, recv_sem=recv,
            device_id=target, device_id_type=MESH,
        )

    barrier = pltpu.get_barrier_semaphore()
    near = [peer(off, r) for off in range(-2, 3) for r in range(4) if (off, r) != (0, 0)]
    for target in near + [peer(-REACH, 0), peer(REACH, 0)]:
        pl.semaphore_signal(barrier, inc=1, device_id=target, device_id_type=MESH)

    def quarter(r):
        return 2 * sides[r // 2] + cores[r % 2]

    def load(i):
        part = pl.ds(pl.multiple_of(i * TILE, TILE), TILE)
        return pltpu.make_async_copy(samples.at[part], x.at[part], in_sem.at[i])

    def load_basis(n, r):
        part = pl.ds(pl.multiple_of(256 * quarter(r), 256), 256)
        return pltpu.make_async_copy(basis.at[:, part], b.at[n], b_sem.at[n])

    ids = [
        pltpu.make_async_copy(shot_ref, shot_ids, id_sem.at[0]),
        pltpu.make_async_copy(recv_ref, recv_ids, id_sem.at[1]),
    ]
    for copy in ids:
        copy.start()
    order = (3, 2, 1, 0)
    load_basis(0, order[0]).start()
    for i in range(tiles):
        load(i).start()
    for n in range(1, 4):
        load_basis(n, order[n]).start()

    for copy in ids:
        copy.wait()
    slot = lax.broadcasted_iota(jnp.int32, (1, rows), 1)
    live = slot < count_ref[0]
    sj, srow = local_rows(shot_ids[...], live, group, core, SHOT)
    rj, rrow = local_rows(recv_ids[...], live, group, core, RECV)
    srow = jnp.where(live, sj * SHOT + srow, -1)
    rrow = jnp.where(live, rj * RECV + rrow, -1)
    for i in range(tiles):
        cols = slice(i * TILE, (i + 1) * TILE)
        ident = lax.broadcasted_iota(jnp.int32, (4 * SHOT, TILE), 0)
        w[: 4 * SHOT, cols] = (ident == srow[:, cols]).astype(F32).astype(BF16)
        ident = lax.broadcasted_iota(jnp.int32, (4 * RECV, TILE), 0)
        w[4 * SHOT :, cols] = (ident == rrow[:, cols]).astype(F32).astype(BF16)
    cacc[...] = jnp.zeros_like(cacc)
    racc[...] = jnp.zeros_like(racc)

    def tally(i, _):
        part = pl.ds(pl.multiple_of(i * TILE, TILE), TILE)
        ws, wr = w[: 4 * SHOT, part], w[4 * SHOT :, part]
        cacc[...] += lax.dot_general(ws, wr, NT, preferred_element_type=F32)
        racc[...] += lax.dot_general(wr, ws, NT, preferred_element_type=F32)
        return 0

    lax.fori_loop(0, tiles, tally, 0)
    for j in range(4):
        for st in range(4):
            top = j * SHOT + 8 * st
            cmsg[j, st, 0:8] = cacc[top : top + 8, 0:128]
            cmsg[j, st, 8:16] = cacc[top : top + 8, 128:256]
            top = j * RECV + 16 * st
            cmsg[j, st, 16:32] = racc[top : top + 16, :]
    csr[...] = jnp.zeros_like(csr)
    crs[...] = jnp.zeros_like(crs)

    def count_copy(n):
        (off, j), r = window[n // 4], n % 4
        to = landing(off, r)
        return remote(
            cmsg.at[j, quarter(r)], cin.at[to], c_send.at[n], c_recv.at[to], peer(off, r)
        )

    lane = lax.broadcasted_iota(jnp.int32, (TILE, 128), 1)
    lane8 = lax.broadcasted_iota(jnp.int32, (8, 128), 1)
    sine, norm = odd

    def nyquist(i):
        part = slice(i * TILE, (i + 1) * TILE)
        even_odd = x[part, 0:128].astype(F32)
        for v in range(1, x.shape[1] // 128):
            even_odd += x[part, 128 * v : 128 * v + 128].astype(F32)
        odds = jnp.sum(jnp.where(lane % 2 == 1, even_odd, 0.0), axis=1, keepdims=True)
        evens = jnp.sum(jnp.where(lane % 2 == 1, 0.0, even_odd), axis=1, keepdims=True)
        re, im = (evens - odds) * norm, odds * sine
        return jnp.log(jnp.broadcast_to(re * re + im * im, (TILE, 128)) + FLOOR)

    def log_spectra(n):
        load_basis(n, order[n]).wait()
        first = pl.multiple_of(128 * quarter(order[n]), 128)
        acc[...] = jnp.zeros_like(acc)
        for i in range(tiles):
            if n == 0:
                load(i).wait()
            part = slice(i * TILE, (i + 1) * TILE)
            y = jnp.dot(x[part], b[n], preferred_element_type=F32)
            re, im = y[:, :128], y[:, 128:]
            value = jnp.log(re * re + im * im + FLOOR)
            spec[pl.ds(first, 128), part] = jnp.transpose(value)
            pieces = list(split(value))
            if n == 0:
                value = nyquist(i)
                spec[512:520, part] = jnp.transpose(value)[0:8]
                hi, lo = split(value)
                pieces.append(jnp.where(lane == 0, hi.astype(F32), lo.astype(F32)).astype(BF16))
            width = 128 * len(pieces)
            acc[:, :width] += jnp.dot(
                w[:, part], jnp.concatenate(pieces, axis=1), preferred_element_type=F32
            )
        for j in range(4):
            for top, size, to in ((j * SHOT, SHOT, 0), (4 * SHOT + j * RECV, RECV, SHOT)):
                msgs[n, j, to : to + size] = (
                    acc[top : top + size, 0:128] + acc[top : top + size, 128:256]
                )
        if n == 0:
            both = acc[:, 256:384]
            both = both + pltpu.roll(both, 127, 1)
            line = [
                jnp.broadcast_to(jnp.transpose(both[128 * v : 128 * v + 128])[0:1], (8, 128))
                for v in range(3)
            ]
            for j in range(4):
                shots = pltpu.roll(line[0], (128 - SHOT * j) % 128, 1)
                recvs = pltpu.roll(line[1 + j // 2], (SHOT + 128 - RECV * (j % 2)) % 128, 1)
                ends = jnp.where(lane8 < SHOT, shots, recvs)
                ends = jnp.where(lane8 < SHOT + RECV, ends, 0.0)
                for m in range(4):
                    msgs[m, j, SHOT + RECV : MSG] = ends

    def sum_copy(n, which):
        (off, j), r = window[which], order[n]
        to = landing(off, r)
        return remote(
            msgs.at[n, j], inbox.at[to], p_send.at[4 * n + which], p_recv.at[to], peer(off, r)
        )

    def sum_copies(n):
        return [sum_copy(n, which) for which in range(4) if (which, order[n]) != (0, 0)]

    def send_sums(n):
        for copy in sum_copies(n):
            copy.start()
        if order[n] == 0:
            inbox[0] = msgs[n, 2 - core]

    def senders():
        yield from ((r, peer(0, r)) for r in range(1, 4))
        for base, off in ((4, -1), (8, 1)):
            yield from ((base + r, peer(off, r)) for r in range(4))
        for base, off in ((12, 2), (14, -2)):
            yield from ((base + r1, edge_peer(off, r1)) for r1 in range(2))

    def arrived(buf, send, recv):
        for n, source in senders():
            remote(buf.at[n], buf.at[n], send.at[n], recv.at[n], source).wait_recv()

    def member_copy(r):
        return remote(cg.at[s], cg.at[s], g_send.at[r], g_recv.at[r], peer(0, r))

    def share_counts():
        arrived(cin, c_send, c_recv)
        shots = jnp.zeros((8, 512), F32)
        recvs = jnp.zeros((16, 256), F32)
        for place in range(4):
            far = {0: 14, 3: 12}
            if place in far:
                base, c = (4, core) if place == 0 else (8, 1 - core)
                part = cin[far[place]] + cin[far[place] + 1]
                part = part + cin[base + c] + cin[base + 2 + c]
            else:
                low, high = (4, 0) if place == 1 else (0, 8)
                part = cin[low + 1 - core] + cin[low + 3 - core]
                part = part + cin[high + core] + cin[high + 2 + core]
            wide = jnp.concatenate([part[0:8], part[8:16], jnp.zeros((8, 256), F32)], axis=1)
            shots += pltpu.roll(wide, RECV * place, 1) if place else wide
            wide = jnp.concatenate([part[16:32], jnp.zeros((16, 128), F32)], axis=1)
            recvs += pltpu.roll(wide, SHOT * place, 1) if place else wide
        for v in range(4):
            cg[s, 8 * v : 8 * v + 8] = shots[:, 128 * v : 128 * v + 128]
        for v in range(2):
            cg[s, 32 + 16 * v : 48 + 16 * v] = recvs[:, 128 * v : 128 * v + 128]
        for r in range(1, 4):
            member_copy(r).start()

    def take_counts():
        for r in range(1, 4):
            st = quarter(r)
            remote(cg.at[st], cg.at[st], g_send.at[r], g_recv.at[r], peer(0, r)).wait_recv()
        for st in range(4):
            for v in range(4):
                csr[8 * st : 8 * st + 8, 128 * v : 128 * v + 128] = cg[st, 8 * v : 8 * v + 8]
            for v in range(2):
                crs[16 * st : 16 * st + 16, 128 * v : 128 * v + 128] = cg[
                    st, 32 + 16 * v : 48 + 16 * v
                ]

    log_spectra(0)
    pl.semaphore_wait(barrier, 21)
    for n in range(1, 16):
        count_copy(n).start()
    cin[0] = cmsg[2 - core, s]
    send_sums(0)
    log_spectra(1)
    send_sums(1)
    share_counts()
    log_spectra(2)
    send_sums(2)
    take_counts()
    log_spectra(3)
    send_sums(3)

    shot_counts = jnp.sum(csr[0:SHOT], axis=1, keepdims=True) + DAMP
    recv_counts = jnp.sum(crs[0:RECV], axis=1, keepdims=True) + DAMP

    def matmul(p, q):
        return jnp.dot(p, q, precision=HIGH, preferred_element_type=F32)

    def matmul_nt(p, q):
        return lax.dot_general(p, q, NT, precision=HIGH, preferred_element_type=F32)

    shot_line = matmul_nt(jnp.ones((8, 512), F32), csr[...]) + DAMP
    recv_line = matmul_nt(jnp.ones((8, 256), F32), crs[...]) + DAMP
    for buf, size in ((s1, SMSG), (r1, RMSG), (s2, SMSG)):
        buf[7] = jnp.zeros((size, 128), F32)

    arrived(inbox, p_send, p_recv)
    total = inbox[0]
    for n in range(1, 16):
        total = total + inbox[n]
    shot_sum = total[0:SHOT]
    recv_sum = total[SHOT : SHOT + RECV]
    ends = total[SHOT + RECV : MSG]
    shot_end = jnp.where(lane8 < SHOT, ends, 0.0)
    recv_end = jnp.where(lane8 < RECV, pltpu.roll(ends, 128 - SHOT, 1), 0.0)

    def spread_copy(buf, send, recv, off):
        return remote(
            buf.at[3], buf.at[3 - off], send.at[3 - off], recv.at[3 - off], peer(off, 0)
        )

    offsets = (3, -3, 2, -2, 1, -1)

    def spread(buf, send, recv):
        for off in offsets:
            spread_copy(buf, send, recv, off).start()

    def gathered(buf, send, recv):
        for off in offsets:
            spread_copy(buf, send, recv, off).wait_recv()

    def shot_matrix(buf):
        main = buf[:, 0:SHOT].reshape(8 * SHOT, 128)
        line = [jnp.zeros((8, 128), F32) for _ in range(2)]
        for n in range(7):
            piece = buf[n, SHOT:SMSG]
            line[n // 4] += pltpu.roll(piece, SHOT * (n % 4), 1) if n % 4 else piece
        return main, jnp.concatenate(line, axis=1)

    def recv_matrix(buf):
        main = buf[:, 0:RECV].reshape(8 * RECV, 128)
        line = [jnp.zeros((8, 128), F32) for _ in range(4)]
        for n in range(7):
            piece = buf[n, RECV:RMSG]
            line[n // 2] += pltpu.roll(piece, RECV, 1) if n % 2 else piece
        return main, jnp.concatenate(line, axis=1)

    s1[3, 0:SHOT] = shot_sum / shot_counts
    s1[3, SHOT:SMSG] = shot_end / shot_line
    spread(s1, s1_send, s1_recv)
    gathered(s1, s1_send, s1_recv)

    main, line = shot_matrix(s1)
    r1[3, 0:RECV] = (recv_sum - matmul(crs[0:RECV], main)) / recv_counts
    r1[3, RECV:RMSG] = (recv_end - matmul_nt(line, crs[...])) / recv_line
    spread(r1, r1_send, r1_recv)
    gathered(r1, r1_send, r1_recv)

    main, line = recv_matrix(r1)
    s2[3, 0:SHOT] = (shot_sum - matmul(csr[0:SHOT], main)) / shot_counts
    s2[3, SHOT:SMSG] = (shot_end - matmul_nt(line, csr[...])) / shot_line
    spread(s2, s2_send, s2_recv)

    def publications(src, first, size, send, recv):
        rows = pl.ds(first, size)
        for off in (0, -1, 1):
            for r in range(4):
                if (off, r) != (0, 0):
                    n = {0: 0, -1: 8, 1: 4}[off] + r
                    j = 2 - off - cores[r % 2]
                    yield remote(src, table.at[s, j, rows], send.at[n], recv.at[n], peer(off, r))
        for r1 in range(2):
            for n, off, j, c in ((12 + r1, 2, 0, core), (14 + r1, -2, 3, 1 - core)):
                yield remote(
                    src, table.at[s, j, rows], send.at[n], recv.at[12 + 2 * r1 + c], edge_peer(off, r1)
                )

    def publish(*what):
        for copy in publications(*what):
            copy.start()

    def published(src, first, size, send, recv):
        rows = pl.ds(first, size)
        for base, (off, j) in zip((0, 4, 8, 12), window):
            for r in range(4):
                if (off, r) != (0, 0):
                    remote(
                        src, table.at[quarter(r), j, rows], send.at[base + r], recv.at[base + r],
                        peer(off, r),
                    ).wait_recv()

    shot_terms = (s2.at[3], 0, SMSG, ts_send, ts_recv)
    recv_terms = (r2, SMSG, RMSG, tr_send, tr_recv)
    publish(*shot_terms)
    table[s, 2 - core, 0:SMSG] = s2[3]
    gathered(s2, s2_send, s2_recv)

    main, line = shot_matrix(s2)
    r2[0:RECV] = (recv_sum - matmul(crs[0:RECV], main)) / recv_counts
    r2[RECV:RMSG] = (recv_end - matmul_nt(line, crs[...])) / recv_line
    publish(*recv_terms)
    table[s, 2 - core, SMSG : SMSG + RMSG] = r2[...]

    for n in range(1, 16):
        count_copy(n).wait_send()
    for n in range(4):
        for copy in sum_copies(n):
            copy.wait_send()
    for r in range(1, 4):
        member_copy(r).wait_send()
    for off in offsets:
        spread_copy(s1, s1_send, s1_recv, off).wait_send()
        spread_copy(r1, r1_send, r1_recv, off).wait_send()
        spread_copy(s2, s2_send, s2_recv, off).wait_send()
    for what in (shot_terms, recv_terms):
        for copy in publications(*what):
            copy.wait_send()
    for what in (shot_terms, recv_terms):
        published(*what)


def solve(basis, odd, shot_id, recv_id, counts, samples):
    rows, nsamp = samples.shape
    dma = pltpu.SemaphoreType.DMA
    vmem = pl.BlockSpec(memory_space=pltpu.VMEM)
    hbm = pl.BlockSpec(memory_space=pltpu.HBM)
    return pl.pallas_call(
        functools.partial(solve_kernel, odd),
        out_shape=(
            jax.ShapeDtypeStruct((nsamp // 2 + 8, rows), F32),
            jax.ShapeDtypeStruct((4 * (SHOT + RECV), rows), BF16),
            jax.ShapeDtypeStruct((4, 4, SMSG + RMSG, 128), F32),
        ),
        in_specs=[hbm, hbm, pl.BlockSpec(memory_space=pltpu.SMEM), hbm, hbm],
        out_specs=(vmem, vmem, vmem),
        scratch_shapes=[
            pltpu.VMEM((rows, nsamp), BF16),
            pltpu.VMEM((4, nsamp, 256), BF16),
            pltpu.VMEM((1, rows), jnp.int32),
            pltpu.VMEM((1, rows), jnp.int32),
            pltpu.VMEM((4 * (SHOT + RECV), 384), F32),
            pltpu.VMEM((4 * SHOT, 4 * RECV), F32),
            pltpu.VMEM((4 * RECV, 4 * SHOT), F32),
            pltpu.VMEM((4, 4, MSG, 128), F32),
            pltpu.VMEM((4, 4, 32, 128), F32),
            pltpu.VMEM((16, MSG, 128), F32),
            pltpu.VMEM((16, 32, 128), F32),
            pltpu.VMEM((4, 64, 128), F32),
            pltpu.VMEM((128, 8 * RECV), F32),
            pltpu.VMEM((128, 8 * SHOT), F32),
            pltpu.VMEM((8, SMSG, 128), F32),
            pltpu.VMEM((8, RMSG, 128), F32),
            pltpu.VMEM((8, SMSG, 128), F32),
            pltpu.VMEM((RMSG, 128), F32),
            dma((rows // TILE,)),
            dma((4,)),
            dma((2,)),
            dma((16,)), dma((16,)),
            dma((4,)), dma((4,)),
            dma((16,)), dma((16,)),
            dma((7,)), dma((7,)),
            dma((7,)), dma((7,)),
            dma((7,)), dma((7,)),
            dma((16,)), dma((16,)),
            dma((16,)), dma((16,)),
        ],
        compiler_params=pltpu.CompilerParams(
            collective_id=0, has_side_effects=True, vmem_limit_bytes=32 * 2**20
        ),
        cost_estimate=pl.CostEstimate(
            flops=9 * 10**9, bytes_accessed=16 * 10**6, transcendentals=2 * 10**6
        ),
    )(shot_id, recv_id, counts, samples, basis)


def residual_kernel(count_ref, shot_owner, recv_owner, spec, w, table, out, shot_out, recv_out, t):
    step = pl.program_id(0)
    d, side, group, core = place()
    s = 2 * side + core
    width = 4 * (SHOT + RECV)

    @pl.when(step == 0)
    def _():
        def put(first, value):
            hi, lo = split(value)
            t[first : first + value.shape[0], 0:width] = hi
            t[first : first + value.shape[0], width : 2 * width] = lo

        for k in range(4):
            shots = [table[k, j, 0:SHOT] for j in range(4)]
            recvs = [table[k, j, SMSG : SMSG + RECV] for j in range(4)]
            put(128 * k, jnp.transpose(jnp.concatenate(shots + recvs, axis=0)))
        shots = [table[0, j, SHOT:SMSG] for j in range(4)]
        recvs = [table[0, j, SMSG + RECV : SMSG + RMSG] for j in range(4)]
        line = shots[0]
        for j in range(1, 4):
            line = line + pltpu.roll(shots[j], SHOT * j, 1)
        lines = [line]
        for j in range(0, 4, 2):
            lines.append(recvs[j] + pltpu.roll(recvs[j + 1], RECV, 1))
        put(512, jnp.concatenate(lines, axis=1))

        j = 2 - core
        blank = jnp.zeros((120, 128), F32)
        ends_s = jnp.transpose(jnp.concatenate([table[0, j, SHOT:SMSG], blank], axis=0))
        ends_r = jnp.transpose(
            jnp.concatenate([table[0, j, SMSG + RECV : SMSG + RMSG], blank], axis=0)
        )
        for owner, owned, first, ends, dst in (
            (shot_owner, 8, 0, ends_s, shot_out),
            (recv_owner, 16, SMSG, ends_r, recv_out),
        ):
            top = pl.multiple_of(first + owned * s, 8)
            index = lax.broadcasted_iota(jnp.int32, (owned, 1), 0)
            pieces = [table[k, j, pl.ds(top, owned)] for k in range(4)]
            end = jnp.zeros((owned, 128), F32)
            for st in range(4):
                end = jnp.where(s == st, ends[owned * st : owned * st + owned], end)
            pieces.append(end)
            for k in range(5):
                value = jnp.zeros((owned, 128), F32)
                for i in range(owned):
                    row = owner[owned * d + i] - owned * d
                    value = jnp.where(index == row, pieces[k][i : i + 1], value)
                if k < 4:
                    dst[:, 128 * k : 128 * k + 128] = value
                else:
                    dst[:, 512:513] = value[:, 0:1]

    part = pl.ds(pl.multiple_of(step * LANES, LANES), LANES)
    hot = w[:, part]
    terms = jnp.dot(t[...], jnp.concatenate([hot, hot], axis=0), preferred_element_type=F32)
    live = lax.broadcasted_iota(jnp.int32, (1, LANES), 1) < count_ref[0] - step * LANES
    out[...] = (jnp.where(live, spec[:, part], 0.0) - terms)[0 : out.shape[0]]


def residuals(counts, shot_owner, recv_owner, spec, w, table):
    rows = spec.shape[1]
    smem = pl.BlockSpec(memory_space=pltpu.SMEM)
    vmem = pl.BlockSpec(memory_space=pltpu.VMEM)
    return pl.pallas_call(
        residual_kernel,
        grid=(rows // LANES,),
        out_shape=(
            jax.ShapeDtypeStruct((513, rows), F32),
            jax.ShapeDtypeStruct((8, 513), F32),
            jax.ShapeDtypeStruct((16, 513), F32),
        ),
        in_specs=[smem, smem, smem, vmem, vmem, vmem],
        out_specs=(
            pl.BlockSpec((513, LANES), lambda i: (0, i)),
            pl.BlockSpec((8, 513), lambda i: (0, 0)),
            pl.BlockSpec((16, 513), lambda i: (0, 0)),
        ),
        scratch_shapes=[pltpu.VMEM((520, 8 * (SHOT + RECV)), BF16)],
        compiler_params=pltpu.CompilerParams(vmem_limit_bytes=24 * 2**20),
        cost_estimate=pl.CostEstimate(
            flops=3 * 10**9, bytes_accessed=10 * 10**6, transcendentals=0
        ),
    )(counts, shot_owner, recv_owner, spec, w, table)


def shards(basis, odd, samples, shot_id, recv_id, shot_owner, recv_owner, counts):
    rows = samples.shape[0]
    shot_id, recv_id = shot_id.reshape(1, rows), recv_id.reshape(1, rows)
    shot_id, recv_id, samples, basis = (
        pltpu.with_memory_space_constraint(a, pltpu.HBM) for a in (shot_id, recv_id, samples, basis)
    )
    spec, w, table = solve(basis, odd, shot_id, recv_id, counts, samples)
    residual, shots, recvs = residuals(counts, shot_owner, recv_owner, spec, w, table)
    return shots, recvs, residual.T


def solution(mesh):
    basis, odd = basis_table(1024)

    def run(*args):
        return shards(jnp.asarray(basis), odd, *args)

    return jax.shard_map(
        run,
        mesh=mesh,
        in_specs=(
            P(("tile", "block"), None),
            P(("tile", "block")),
            P(("tile", "block")),
            P(),
            P(),
            P(("tile", "block")),
        ),
        out_specs=(
            P(("tile", "block"), None),
            P(("tile", "block"), None),
            P(("tile", "block"), None),
        ),
        check_vma=False,
    )
```

time: 100 us -> 82.5 us (0.82)
  the two profiles are of different devices: /device:TPU:35 before, /device:TPU:1 now
where the time goes in v2:
time: 82.5 us; the launch traced here: 82.3 us
  Pallas kernels  81 us (98%)
  between operations  1.32 us (2%)
    pallas_call x1, Pallas kernels, solve(): pl.pallas_call(functools.partial(solve_kernel, odd), out_shape=(jax.Shape...  74.5 us
    pallas_call x1, Pallas kernels, residuals(): pl.pallas_call(residual_kernel, grid=(rows // LANES,), out_shape=(jax.Sha...  6.53 us

profile of v2, /device:TPU:1, one launch (start us, length us, event | category | flops | bytes accessed | tf_op | source)
XLA Modules:
  0.0 82.3 jit_solution(1664288812185614047)
XLA Ops:
  1.3 0.0 copy-start
  1.3 0.0 copy-start.1
  1.3 74.5 %shard_map.94 = (f32[520,3072]{1,0:T(8,128)S(1)}, bf16[384,3072]{1,0:T(8,128)(2,1)S(1)}, f32[4,4,112,128]{3,2,1,0:T(8,128)S(1)}) custom-call(s32[1,3072]{1,0:T(1,128)} %bitcast.3, s32[1,3072]{1,0:T(1,128)} %bitcast.4, s32[1]{0:T(128)S(6)} %copy.10.count_ref, bf16[3072,1024]{1,0:T(8,128)(2,1)} %samples.1, bf16[1024,1024]{1,0:T(8,128)(2,1)} %constant.2.clone.basis), custom_call_target="tpu_custom_call" | custom-call | flops 8999999488 | bytes 16000000 | tf_op jit(solution)/shard_map/pallas_call | solution.py:461
  75.8 0.0 copy-done
  75.8 0.0 copy-done.1
  75.8 6.5 %shard_map.95 = (f32[513,3072]{1,0:T(8,128)}, f32[8,513]{1,0:T(8,128)}, f32[16,513]{1,0:T(8,128)}) custom-call(s32[1]{0:T(128)S(6)} %copy.10.count_ref, s32[1024]{0:T(1024)S(1)} %copy-done.1, s32[2048]{0:T(1024)S(1)} %copy-done, f32[520,3072]{1,0:T(8,128)S(1)} %get-tuple-element.9.spec, bf16[384,3072]{1,0:T(8,128)(2,1)S(1)} %get-tuple-element.10.w, ...), custom_call_target="tpu_custom_call" | custom-call | flops 3000000000 | bytes 10000000 | tf_op jit(solution)/shard_map/pallas_call | solution.py:575
Async XLA Ops:
  1.3 74.5 %copy-start = (s32[2048]{0:T(1024)S(1)}, s32[2048]{0:T(1024)}, u32[]{:S(2)}) copy-start(s32[2048]{0:T(1024)} %recv_owner.1) | copy-start | bytes 24580
  1.3 74.5 %copy-start.1 = (s32[1024]{0:T(1024)S(1)}, s32[1024]{0:T(1024)}, u32[]{:S(2)}) copy-start(s32[1024]{0:T(1024)} %shot_owner.1) | copy-start | bytes 12292

commit v3 on v2

--- a/solution.py
+++ b/solution.py
@@ -74,11 +74,11 @@
 
 
 def solve_kernel(
-    odd, shot_ref, recv_ref, count_ref, samples, basis, spec, w, table,
-    x, b, shot_ids, recv_ids, acc, cacc, racc, msgs, cmsg, inbox, cin, cg, csr, crs,
+    odd, shot_ref, recv_ref, count_ref, samples, basis, spec, w, table_s, table_r,
+    x, b, shot_ids, recv_ids, hl, acc, cacc, racc, msgs, cmsg, inbox, cin, cg, csr, crs,
     s1, r1, s2, r2, in_sem, b_sem, id_sem, c_send, c_recv, g_send, g_recv,
     p_send, p_recv, s1_send, s1_recv, r1_send, r1_recv, s2_send, s2_recv,
-    ts_send, ts_recv, tr_send, tr_recv,
+    ts_send, ts_recv, tr_send, tr_recv, fs_send, fs_recv, fr_send, fr_recv,
 ):
     me, side, group, core = place()
     s = 2 * side + core
@@ -203,7 +203,6 @@
     def log_spectra(n):
         load_basis(n, order[n]).wait()
         first = pl.multiple_of(128 * quarter(order[n]), 128)
-        acc[...] = jnp.zeros_like(acc)
         for i in range(tiles):
             if n == 0:
                 load(i).wait()
@@ -212,16 +211,14 @@
             re, im = y[:, :128], y[:, 128:]
             value = jnp.log(re * re + im * im + FLOOR)
             spec[pl.ds(first, 128), part] = jnp.transpose(value)
-            pieces = list(split(value))
+            hl[part, 0:128], hl[part, 128:256] = split(value)
             if n == 0:
                 value = nyquist(i)
                 spec[512:520, part] = jnp.transpose(value)[0:8]
                 hi, lo = split(value)
-                pieces.append(jnp.where(lane == 0, hi.astype(F32), lo.astype(F32)).astype(BF16))
-            width = 128 * len(pieces)
-            acc[:, :width] += jnp.dot(
-                w[:, part], jnp.concatenate(pieces, axis=1), preferred_element_type=F32
-            )
+                hl[part, 256:384] = jnp.where(lane == 0, hi.astype(F32), lo.astype(F32)).astype(BF16)
+        width = 384 if n == 0 else 256
+        acc[:, :width] = jnp.dot(w[...], hl[:, :width], preferred_element_type=F32)
         for j in range(4):
             for top, size, to in ((j * SHOT, SHOT, 0), (4 * SHOT + j * RECV, RECV, SHOT)):
                 msgs[n, j, to : to + size] = (
@@ -317,12 +314,12 @@
     send_sums(0)
     log_spectra(1)
     send_sums(1)
-    share_counts()
     log_spectra(2)
     send_sums(2)
-    take_counts()
+    share_counts()
     log_spectra(3)
     send_sums(3)
+    take_counts()
 
     shot_counts = jnp.sum(csr[0:SHOT], axis=1, keepdims=True) + DAMP
     recv_counts = jnp.sum(crs[0:RECV], axis=1, keepdims=True) + DAMP
@@ -395,45 +392,76 @@
     s2[3, SHOT:SMSG] = (shot_end - matmul_nt(line, csr[...])) / shot_line
     spread(s2, s2_send, s2_recv)
 
-    def publications(src, first, size, send, recv):
-        rows = pl.ds(first, size)
-        for off in (0, -1, 1):
-            for r in range(4):
+    def publications(src, table, send, recv):
+        for off in (2, -2, 1, -1, 0):
+            for r in (2, 0):
                 if (off, r) != (0, 0):
-                    n = {0: 0, -1: 8, 1: 4}[off] + r
-                    j = 2 - off - cores[r % 2]
-                    yield remote(src, table.at[s, j, rows], send.at[n], recv.at[n], peer(off, r))
-        for r1 in range(2):
-            for n, off, j, c in ((12 + r1, 2, 0, core), (14 + r1, -2, 3, 1 - core)):
-                yield remote(
-                    src, table.at[s, j, rows], send.at[n], recv.at[12 + 2 * r1 + c], edge_peer(off, r1)
-                )
+                    n = 5 * (r // 2) + 2 - off
+                    yield remote(
+                        src, table.at[core, side, 2 - off], send.at[n], recv.at[n], peer(off, r)
+                    )
+
+    def hand_on(table, send, recv, r, off):
+        n = 5 * (r // 2) + 2 + off
+        block = table.at[core, sides[r // 2], 2 + off]
+        return remote(block, block, send.at[n], recv.at[n], peer(0, 1))
+
+    def relay(src, table, send, recv, send_on, recv_on):
+        for r in (0, 2):
+            for off in (0, 1, -1, 2, -2):
+                if (off, r) != (0, 0):
+                    n = 5 * (r // 2) + 2 + off
+                    remote(
+                        src, table.at[core, sides[r // 2], 2 + off], send.at[n], recv.at[n],
+                        peer(off, r),
+                    ).wait_recv()
+                hand_on(table, send_on, recv_on, r, off).start()
+
+    def relayed(table, send, recv):
+        for r in (0, 2):
+            for off in (0, 1, -1, 2, -2):
+                n = 5 * (r // 2) + 2 + off
+                block = table.at[1 - core, sides[r // 2], 2 + off]
+                remote(block, block, send.at[n], recv.at[n], peer(0, 1)).wait_recv()
+
+    shot_terms = (s2.at[3], table_s, ts_send, ts_recv)
+    recv_terms = (r2, table_r, tr_send, tr_recv)
 
     def publish(*what):
         for copy in publications(*what):
             copy.start()
 
-    def published(src, first, size, send, recv):
-        rows = pl.ds(first, size)
-        for base, (off, j) in zip((0, 4, 8, 12), window):
-            for r in range(4):
-                if (off, r) != (0, 0):
-                    remote(
-                        src, table.at[quarter(r), j, rows], send.at[base + r], recv.at[base + r],
-                        peer(off, r),
-                    ).wait_recv()
-
-    shot_terms = (s2.at[3], 0, SMSG, ts_send, ts_recv)
-    recv_terms = (r2, SMSG, RMSG, tr_send, tr_recv)
     publish(*shot_terms)
-    table[s, 2 - core, 0:SMSG] = s2[3]
+    table_s[core, side, 2] = s2[3]
     gathered(s2, s2_send, s2_recv)
 
     main, line = shot_matrix(s2)
     r2[0:RECV] = (recv_sum - matmul(crs[0:RECV], main)) / recv_counts
     r2[RECV:RMSG] = (recv_end - matmul_nt(line, crs[...])) / recv_line
     publish(*recv_terms)
-    table[s, 2 - core, SMSG : SMSG + RMSG] = r2[...]
+    table_r[core, side, 2] = r2[...]
+
+    relay(*shot_terms, fs_send, fs_recv)
+    relayed(table_s, fs_send, fs_recv)
+
+    def both_parts(value):
+        return jnp.concatenate(split(value), axis=1)
+
+    lifted = []
+    for k in range(4):
+        terms = jnp.concatenate([table_s[k % 2, k // 2, j + core, 0:SHOT] for j in range(4)], axis=0)
+        lifted.append(both_parts(jnp.transpose(terms)))
+    line = table_s[0, 0, core, SHOT:SMSG]
+    for j in range(1, 4):
+        line = line + pltpu.roll(table_s[0, 0, j + core, SHOT:SMSG], SHOT * j, 1)
+    lifted.append(both_parts(line))
+    for i in range(tiles):
+        part = slice(i * TILE, (i + 1) * TILE)
+        hot = jnp.concatenate([w[0 : 4 * SHOT, part]] * 2, axis=0)
+        for k in range(5):
+            bins = slice(128 * k, min(128 * k + 128, spec.shape[0]))
+            terms = jnp.dot(lifted[k], hot, preferred_element_type=F32)
+            spec[bins, part] = jnp.where(live[:, part], spec[bins, part], 0.0) - terms
 
     for n in range(1, 16):
         count_copy(n).wait_send()
@@ -449,8 +477,12 @@
     for what in (shot_terms, recv_terms):
         for copy in publications(*what):
             copy.wait_send()
-    for what in (shot_terms, recv_terms):
-        published(*what)
+    relay(*recv_terms, fr_send, fr_recv)
+    for r in (0, 2):
+        for off in range(-2, 3):
+            hand_on(table_s, fs_send, fs_recv, r, off).wait_send()
+            hand_on(table_r, fr_send, fr_recv, r, off).wait_send()
+    relayed(table_r, fr_send, fr_recv)
 
 
 def solve(basis, odd, shot_id, recv_id, counts, samples):
@@ -463,15 +495,17 @@
         out_shape=(
             jax.ShapeDtypeStruct((nsamp // 2 + 8, rows), F32),
             jax.ShapeDtypeStruct((4 * (SHOT + RECV), rows), BF16),
-            jax.ShapeDtypeStruct((4, 4, SMSG + RMSG, 128), F32),
+            jax.ShapeDtypeStruct((2, 2, 5, SMSG, 128), F32),
+            jax.ShapeDtypeStruct((2, 2, 5, RMSG, 128), F32),
         ),
         in_specs=[hbm, hbm, pl.BlockSpec(memory_space=pltpu.SMEM), hbm, hbm],
-        out_specs=(vmem, vmem, vmem),
+        out_specs=(vmem, vmem, vmem, vmem),
         scratch_shapes=[
             pltpu.VMEM((rows, nsamp), BF16),
             pltpu.VMEM((4, nsamp, 256), BF16),
             pltpu.VMEM((1, rows), jnp.int32),
             pltpu.VMEM((1, rows), jnp.int32),
+            pltpu.VMEM((rows, 384), BF16),
             pltpu.VMEM((4 * (SHOT + RECV), 384), F32),
             pltpu.VMEM((4 * SHOT, 4 * RECV), F32),
             pltpu.VMEM((4 * RECV, 4 * SHOT), F32),
@@ -495,8 +529,10 @@
             dma((7,)), dma((7,)),
             dma((7,)), dma((7,)),
             dma((7,)), dma((7,)),
-            dma((16,)), dma((16,)),
-            dma((16,)), dma((16,)),
+            dma((10,)), dma((10,)),
+            dma((10,)), dma((10,)),
+            dma((10,)), dma((10,)),
+            dma((10,)), dma((10,)),
         ],
         compiler_params=pltpu.CompilerParams(
             collective_id=0, has_side_effects=True, vmem_limit_bytes=32 * 2**20
@@ -507,11 +543,11 @@
     )(shot_id, recv_id, counts, samples, basis)
 
 
-def residual_kernel(count_ref, shot_owner, recv_owner, spec, w, table, out, shot_out, recv_out, t):
+def residual_kernel(shot_owner, recv_owner, spec, w, table_s, table_r, out, shot_out, recv_out, t):
     step = pl.program_id(0)
     d, side, group, core = place()
     s = 2 * side + core
-    width = 4 * (SHOT + RECV)
+    width = 4 * RECV
 
     @pl.when(step == 0)
     def _():
@@ -521,32 +557,22 @@
             t[first : first + value.shape[0], width : 2 * width] = lo
 
         for k in range(4):
-            shots = [table[k, j, 0:SHOT] for j in range(4)]
-            recvs = [table[k, j, SMSG : SMSG + RECV] for j in range(4)]
-            put(128 * k, jnp.transpose(jnp.concatenate(shots + recvs, axis=0)))
-        shots = [table[0, j, SHOT:SMSG] for j in range(4)]
-        recvs = [table[0, j, SMSG + RECV : SMSG + RMSG] for j in range(4)]
-        line = shots[0]
-        for j in range(1, 4):
-            line = line + pltpu.roll(shots[j], SHOT * j, 1)
-        lines = [line]
-        for j in range(0, 4, 2):
-            lines.append(recvs[j] + pltpu.roll(recvs[j + 1], RECV, 1))
+            terms = [table_r[k % 2, k // 2, j + core, 0:RECV] for j in range(4)]
+            put(128 * k, jnp.transpose(jnp.concatenate(terms, axis=0)))
+        ends = [table_r[0, 0, j + core, RECV:RMSG] for j in range(4)]
+        lines = [ends[j] + pltpu.roll(ends[j + 1], RECV, 1) for j in range(0, 4, 2)]
         put(512, jnp.concatenate(lines, axis=1))
 
-        j = 2 - core
         blank = jnp.zeros((120, 128), F32)
-        ends_s = jnp.transpose(jnp.concatenate([table[0, j, SHOT:SMSG], blank], axis=0))
-        ends_r = jnp.transpose(
-            jnp.concatenate([table[0, j, SMSG + RECV : SMSG + RMSG], blank], axis=0)
-        )
-        for owner, owned, first, ends, dst in (
-            (shot_owner, 8, 0, ends_s, shot_out),
-            (recv_owner, 16, SMSG, ends_r, recv_out),
+        ends_s = jnp.transpose(jnp.concatenate([table_s[0, 0, 2, SHOT:SMSG], blank], axis=0))
+        ends_r = jnp.transpose(jnp.concatenate([table_r[0, 0, 2, RECV:RMSG], blank], axis=0))
+        for owner, owned, table, ends, dst in (
+            (shot_owner, 8, table_s, ends_s, shot_out),
+            (recv_owner, 16, table_r, ends_r, recv_out),
         ):
-            top = pl.multiple_of(first + owned * s, 8)
+            top = pl.multiple_of(owned * s, 8)
             index = lax.broadcasted_iota(jnp.int32, (owned, 1), 0)
-            pieces = [table[k, j, pl.ds(top, owned)] for k in range(4)]
+            pieces = [table[k % 2, k // 2, 2, pl.ds(top, owned)] for k in range(4)]
             end = jnp.zeros((owned, 128), F32)
             for st in range(4):
                 end = jnp.where(s == st, ends[owned * st : owned * st + owned], end)
@@ -562,13 +588,12 @@
                     dst[:, 512:513] = value[:, 0:1]
 
     part = pl.ds(pl.multiple_of(step * LANES, LANES), LANES)
-    hot = w[:, part]
+    hot = w[4 * SHOT :, part]
     terms = jnp.dot(t[...], jnp.concatenate([hot, hot], axis=0), preferred_element_type=F32)
-    live = lax.broadcasted_iota(jnp.int32, (1, LANES), 1) < count_ref[0] - step * LANES
-    out[...] = (jnp.where(live, spec[:, part], 0.0) - terms)[0 : out.shape[0]]
-
-
-def residuals(counts, shot_owner, recv_owner, spec, w, table):
+    out[...] = (spec[:, part] - terms)[0 : out.shape[0]]
+
+
+def residuals(shot_owner, recv_owner, spec, w, table_s, table_r):
     rows = spec.shape[1]
     smem = pl.BlockSpec(memory_space=pltpu.SMEM)
     vmem = pl.BlockSpec(memory_space=pltpu.VMEM)
@@ -580,18 +605,18 @@
             jax.ShapeDtypeStruct((8, 513), F32),
             jax.ShapeDtypeStruct((16, 513), F32),
         ),
-        in_specs=[smem, smem, smem, vmem, vmem, vmem],
+        in_specs=[smem, smem, vmem, vmem, vmem, vmem],
         out_specs=(
             pl.BlockSpec((513, LANES), lambda i: (0, i)),
             pl.BlockSpec((8, 513), lambda i: (0, 0)),
             pl.BlockSpec((16, 513), lambda i: (0, 0)),
         ),
-        scratch_shapes=[pltpu.VMEM((520, 8 * (SHOT + RECV)), BF16)],
+        scratch_shapes=[pltpu.VMEM((spec.shape[0], 8 * RECV), BF16)],
         compiler_params=pltpu.CompilerParams(vmem_limit_bytes=24 * 2**20),
         cost_estimate=pl.CostEstimate(
             flops=3 * 10**9, bytes_accessed=10 * 10**6, transcendentals=0
         ),
-    )(counts, shot_owner, recv_owner, spec, w, table)
+    )(shot_owner, recv_owner, spec, w, table_s, table_r)
 
 
 def shards(basis, odd, samples, shot_id, recv_id, shot_owner, recv_owner, counts):
@@ -600,8 +625,8 @@
     shot_id, recv_id, samples, basis = (
         pltpu.with_memory_space_constraint(a, pltpu.HBM) for a in (shot_id, recv_id, samples, basis)
     )
-    spec, w, table = solve(basis, odd, shot_id, recv_id, counts, samples)
-    residual, shots, recvs = residuals(counts, shot_owner, recv_owner, spec, w, table)
+    spec, w, table_s, table_r = solve(basis, odd, shot_id, recv_id, counts, samples)
+    residual, shots, recvs = residuals(shot_owner, recv_owner, spec, w, table_s, table_r)
     return shots, recvs, residual.T
 
 

time: 82.5 us -> 71.7 us (0.87)
  Pallas kernels: 81 us -> 70.2 us
    pallas_call x1, Pallas kernels: 74.5 us -> 64.3 us  [solve(): pl.pallas_call(functools.partial(solve_kernel, odd), out_shape=(jax.Shape...]
where the time goes in v3:
time: 71.7 us; the launch traced here: 71.6 us
  Pallas kernels  70.2 us (98%)
  between operations  1.32 us (2%)
    pallas_call x1, Pallas kernels, solve(): pl.pallas_call(functools.partial(solve_kernel, odd), out_shape=(jax.Shape...  64.3 us
    pallas_call x1, Pallas kernels, residuals(): pl.pallas_call(residual_kernel, grid=(rows // LANES,), out_shape=(jax.Sha...  5.9 us

profile of v3, /device:TPU:1, one launch (start us, length us, event | category | flops | bytes accessed | tf_op | source)
XLA Modules:
  0.0 71.6 jit_solution(18255774746059652683)
XLA Ops:
  1.3 0.0 copy-start
  1.3 0.0 copy-start.1
  1.3 64.3 %shard_map.94 = (f32[520,3072]{1,0:T(8,128)S(1)}, bf16[384,3072]{1,0:T(8,128)(2,1)S(1)}, f32[2,2,5,40,128]{4,3,2,1,0:T(8,128)S(1)}, f32[2,2,5,72,128]{4,3,2,1,0:T(8,128)S(1)}) custom-call(s32[1,3072]{1,0:T(1,128)} %bitcast.3, s32[1,3072]{1,0:T(1,128)} %bitcast.4, s32[1]{0:T(128)S(6)} %copy.10.count_ref, bf16[3072,1024]{1,0:T(8,128)(2,1)} %samples.1, ...), custom_call_target="tpu_custom_call" | custom-call | flops 8999999488 | bytes 16000000 | tf_op jit(solution)/shard_map/pallas_call | solution.py:493
  65.6 0.0 copy-done
  65.7 0.0 copy-done.1
  65.7 5.9 %shard_map.95 = (f32[513,3072]{1,0:T(8,128)}, f32[8,513]{1,0:T(8,128)}, f32[16,513]{1,0:T(8,128)}) custom-call(s32[1024]{0:T(1024)S(1)} %copy-done.1, s32[2048]{0:T(1024)S(1)} %copy-done, f32[520,3072]{1,0:T(8,128)S(1)} %get-tuple-element.10.spec, bf16[384,3072]{1,0:T(8,128)(2,1)S(1)} %get-tuple-element.11.w, ...), custom_call_target="tpu_custom_call" | custom-call | flops 3000000000 | bytes 10000000 | tf_op jit(solution)/shard_map/pallas_call | solution.py:600
Async XLA Ops:
  1.3 64.4 %copy-start = (s32[2048]{0:T(1024)S(1)}, s32[2048]{0:T(1024)}, u32[]{:S(2)}) copy-start(s32[2048]{0:T(1024)} %recv_owner.1) | copy-start | bytes 24580
  1.3 64.4 %copy-start.1 = (s32[1024]{0:T(1024)S(1)}, s32[1024]{0:T(1024)}, u32[]{:S(2)}) copy-start(s32[1024]{0:T(1024)} %shot_owner.1) | copy-start | bytes 12292

commit v4 on v3

--- a/solution.py
+++ b/solution.py
@@ -21,7 +21,7 @@
 SMSG = SHOT + 8
 RMSG = RECV + 8
 TILE = 1024
-LANES = 512
+LANES = 1024
 MESH = pl.DeviceIdType.MESH
 F32 = jnp.float32
 BF16 = jnp.bfloat16
@@ -168,14 +168,6 @@
         racc[...] += lax.dot_general(wr, ws, NT, preferred_element_type=F32)
         return 0
 
-    lax.fori_loop(0, tiles, tally, 0)
-    for j in range(4):
-        for st in range(4):
-            top = j * SHOT + 8 * st
-            cmsg[j, st, 0:8] = cacc[top : top + 8, 0:128]
-            cmsg[j, st, 8:16] = cacc[top : top + 8, 128:256]
-            top = j * RECV + 16 * st
-            cmsg[j, st, 16:32] = racc[top : top + 16, :]
     csr[...] = jnp.zeros_like(csr)
     crs[...] = jnp.zeros_like(crs)
 
@@ -307,6 +299,14 @@
                 ]
 
     log_spectra(0)
+    lax.fori_loop(0, tiles, tally, 0)
+    for j in range(4):
+        for st in range(4):
+            top = j * SHOT + 8 * st
+            cmsg[j, st, 0:8] = cacc[top : top + 8, 0:128]
+            cmsg[j, st, 8:16] = cacc[top : top + 8, 128:256]
+            top = j * RECV + 16 * st
+            cmsg[j, st, 16:32] = racc[top : top + 16, :]
     pl.semaphore_wait(barrier, 21)
     for n in range(1, 16):
         count_copy(n).start()

time: 71.7 us -> 70.9 us (0.989)
  no operation moved by 1% of the time
where the time goes in v4:
time: 70.9 us; the launch traced here: 70.8 us
  Pallas kernels  69.5 us (98%)
  between operations  1.32 us (2%)
    pallas_call x1, Pallas kernels, solve(): pl.pallas_call(functools.partial(solve_kernel, odd), out_shape=(jax.Shape...  64.2 us
    pallas_call x1, Pallas kernels, residuals(): pl.pallas_call(residual_kernel, grid=(rows // LANES,), out_shape=(jax.Sha...  5.26 us

profile of v4, /device:TPU:1, one launch (start us, length us, event | category | flops | bytes accessed | tf_op | source)
XLA Modules:
  0.0 70.8 jit_solution(13668685810348710551)
XLA Ops:
  1.3 0.0 copy-start
  1.3 0.0 copy-start.1
  1.3 64.2 %shard_map.94 = (f32[520,3072]{1,0:T(8,128)S(1)}, bf16[384,3072]{1,0:T(8,128)(2,1)S(1)}, f32[2,2,5,40,128]{4,3,2,1,0:T(8,128)S(1)}, f32[2,2,5,72,128]{4,3,2,1,0:T(8,128)S(1)}) custom-call(s32[1,3072]{1,0:T(1,128)} %bitcast.3, s32[1,3072]{1,0:T(1,128)} %bitcast.4, s32[1]{0:T(128)S(6)} %copy.10.count_ref, bf16[3072,1024]{1,0:T(8,128)(2,1)} %samples.1, ...), custom_call_target="tpu_custom_call" | custom-call | flops 8999999488 | bytes 16000000 | tf_op jit(solution)/shard_map/pallas_call | solution.py:493
  65.5 0.0 copy-done
  65.5 0.0 copy-done.1
  65.5 5.3 %shard_map.95 = (f32[513,3072]{1,0:T(8,128)}, f32[8,513]{1,0:T(8,128)}, f32[16,513]{1,0:T(8,128)}) custom-call(s32[1024]{0:T(1024)S(1)} %copy-done.1, s32[2048]{0:T(1024)S(1)} %copy-done, f32[520,3072]{1,0:T(8,128)S(1)} %get-tuple-element.10.spec, bf16[384,3072]{1,0:T(8,128)(2,1)S(1)} %get-tuple-element.11.w, ...), custom_call_target="tpu_custom_call" | custom-call | flops 3000000000 | bytes 10000000 | tf_op jit(solution)/shard_map/pallas_call | solution.py:600
Async XLA Ops:
  1.3 64.2 %copy-start = (s32[2048]{0:T(1024)S(1)}, s32[2048]{0:T(1024)}, u32[]{:S(2)}) copy-start(s32[2048]{0:T(1024)} %recv_owner.1) | copy-start | bytes 24580
  1.3 64.2 %copy-start.1 = (s32[1024]{0:T(1024)S(1)}, s32[1024]{0:T(1024)}, u32[]{:S(2)}) copy-start(s32[1024]{0:T(1024)} %shot_owner.1) | copy-start | bytes 12292
